TPU v7x, 256 devices: a whole 4x4x8 slice. The times are simulated.
256 devices in a mesh: band: 32 (over z, x_hi, core), slab: 8 (over x_lo, y).
Axes of the slice: x: 4 (x_hi: 2, x_lo: 2; x = x_hi * 2 + x_lo), y: 4, z: 8, core: 2. Of those that a mesh axis runs over, the one named last changes fastest.
Arguments:
- orbital: float32 [32, 128, 128, 128], P('band', 'slab'), may hold values from -18 to 18
- potential: float32 [128, 128, 128], P('slab', 'band'), may hold values from -4 to 2
Outputs:
- filtered: float32 [32, 128, 128, 128], P('band', 'slab')
All inputs are finite; a program needn't handle non-finite values.
Results may differ from a plain program's by a relative error of at most 0.00002.
Values sent between devices are 32-bit elements; how exact they have to be, the bound alone decides.
No kernel may reach another device: no remote copies, remote signals or barrier semaphores. Data moves between devices by JAX's collectives and lax.ppermute only.
A program may use at most 64 MiB of HBM per device.

v0:
```python
import jax
import jax.numpy as jnp
from jax import lax
from jax.sharding import PartitionSpec as P

DEGREE = 3


COEFS = (
    -5369.0 / 1800.0,
    12.0 / 7.0,
    -15.0 / 56.0,
    10.0 / 189.0,
    -1.0 / 112.0,
    2.0 / 1925.0,
    -1.0 / 16632.0,
)
INVERSE_SQ = 1.0 / 0.64
UPPER_HALF = 10.0
CENTER = 10.0
FLOOR = -5.0


def with_halo(block, sides, width):
    for axis, dim in sides:
        count = lax.axis_size(axis)
        forward = [(i, i + 1) for i in range(count - 1)]
        forward.append((count - 1, 0))
        backward = [(target, source) for source, target in forward]
        low = lax.ppermute(
            lax.slice_in_dim(block, block.shape[dim] - width, None, axis=dim), axis, forward
        )
        high = lax.ppermute(lax.slice_in_dim(block, 0, width, axis=dim), axis, backward)
        block = jnp.concatenate([low, block, high], axis=dim)
    return block


def hamil_padded(padded, vrows):
    count = padded.shape[0] - 12
    center = padded[6 : 6 + count]
    rows_y = center.shape[1]
    cols_z = center.shape[2]
    wrapped = jnp.pad(center, ((0, 0), (6, 6), (6, 6)), mode="wrap")
    total = 3.0 * COEFS[0] * center
    for shift in range(1, 7):
        near = padded[6 - shift : 6 - shift + count] + padded[6 + shift : 6 + shift + count]
        near = (
            near
            + wrapped[:, 6 - shift : 6 - shift + rows_y, 6 : 6 + cols_z]
            + wrapped[:, 6 + shift : 6 + shift + rows_y, 6 : 6 + cols_z]
        )
        near = (
            near
            + wrapped[:, 6 : 6 + rows_y, 6 - shift : 6 - shift + cols_z]
            + wrapped[:, 6 : 6 + rows_y, 6 + shift : 6 + shift + cols_z]
        )
        total = total + COEFS[shift] * near
    return -0.5 * INVERSE_SQ * total + vrows * center


def with_faces(field):
    return with_halo(field, (("slab", 0),), 6)


def shards(orbital, potential):
    vfull = lax.all_gather(potential, "band", axis=1, tiled=True)
    sigma_one = UPPER_HALF / (FLOOR - CENTER)
    gamma = 2.0 / sigma_one
    start = orbital[0]
    older = start
    newer = sigma_one / UPPER_HALF * (hamil_padded(with_faces(older), vfull) - CENTER * older)
    sigma = sigma_one
    for step in range(DEGREE - 1):
        tnext = 1.0 / (gamma - sigma)
        image = hamil_padded(with_faces(newer), vfull)
        fresh = 2.0 * tnext / UPPER_HALF * (image - CENTER * newer) - sigma * tnext * older
        older, newer = (newer, fresh)
        sigma = tnext
    return newer[None]


def solution(mesh):
    placed = (P("band", "slab", None, None), P("slab", "band", None))
    return jax.shard_map(
        shards, mesh=mesh, in_specs=placed, out_specs=P("band", "slab", None, None), check_vma=False
    )
```

profile of v0, /device:TPU:24, one launch (start us, length us, event | category | flops | bytes accessed | tf_op | source)
XLA Modules:
  0.0 165.0 jit_solution(4405136198025808887)
XLA Ops:
  6.5 1.4 copy.6
  7.9 1.8 %copy.11 = f32[1,16,128,128]{3,1,2,0:T(8,128)S(1)} copy(f32[1,16,128,128]{3,2,1,0:T(8,128)} %param.2) | data formatting | bytes 2097152 | tf_op args[0]
  9.9 1.2 collective-permute-start
  11.1 0.9 collective-permute-start.1
  12.4 2.3 %maximum_maximum_fusion = (f32[16,140,134]{2,0,1:T(8,128)S(1)}, f32[16,140,134]{2,0,1:T(8,128)}) fusion(f32[16,6,128]{2,0,1:T(8,128)S(1)} %get-tuple-element.32, f32[16,128,128]{2,0,1:T(8,128)S(1)} %bitcast.11, f32[16,6,128]{2,0,1:T(8,128)S(1)} %get-tuple-element.31, f32[16,140,6]{2,0,1:T(8,128)S(1)} %get-tuple-element.17, ...), kind=kLoop, calls=%fused_computation.60 | loop fusion | flops 1800960 | bytes 3655680 | tf_op jit(solution)/shard_map/jit(_pad)/concatenate | solution.py:43
  14.7 9.0 %collective-permute-done = f32[6,128,128]{2,0,1:T(8,128)} collective-permute-done((f32[6,128,128]{2,0,1:T(8,128)S(1)}, f32[6,128,128]{2,0,1:T(8,128)}, u32[]{:S(2)}, u32[]{:S(2)}) %collective-permute-start) | collective-permute-done | bytes 393248 | tf_op jit(solution)/shard_map/ppermute | solution.py:30
  23.7 3.0 %collective-permute-done.1 = f32[6,128,128]{2,0,1:T(8,128)} collective-permute-done((f32[6,128,128]{2,0,1:T(8,128)S(1)}, f32[6,128,128]{2,0,1:T(8,128)}, u32[]{:S(2)}, u32[]{:S(2)}) %collective-permute-start.1) | collective-permute-done | bytes 393248 | tf_op jit(solution)/shard_map/ppermute | solution.py:33
  26.7 63.7 %all-gather.2.cloned.1.call-done = f32[16,128,128]{2,0,1:T(8,128)} async-done(((f32[16,4,128]{2,0,1:T(8,128)}), f32[16,128,128]{2,0,1:T(8,128)}) %all-gather.2.cloned.1.call-update) | async-done | bytes 1048592 | tf_op jit(solution)/shard_map/all_gather | solution.py:66
  90.4 14.4 %broadcast_multiply_fusion = (f32[16,128,128]{2,0,1:T(8,128)S(1)}, f32[16,128,128]{2,0,1:T(8,128)}) fusion(f32[16,128,128]{2,0,1:T(8,128)S(1)} %bitcast.12, f32[16,128,128]{2,0,1:T(8,128)} %all-gather.2.cloned.1.call-done, f32[16,140,134]{2,0,1:T(8,128)} %get-tuple-element.16, f32[16,140,134]{2,0,1:T(8,128)S(1)} %get-tuple-element.15, ...), kind=kLoop, calls=%fused_computation.331 | loop fusion | flops 19136512 | bytes 17661952 | tf_op jit(solution)/shard_map/mul | solution.py:71
  104.9 0.5 collective-permute-start.2
  105.4 1.6 collective-permute-start.3
  107.5 0.8 maximum_maximum_fusion.1
  108.3 10.8 %collective-permute-done.2 = f32[6,128,128]{2,0,1:T(8,128)S(1)} collective-permute-done((f32[6,128,128]{2,0,1:T(8,128)S(1)}, f32[6,128,128]{2,0,1:T(8,128)S(1)}, u32[]{:S(2)}, u32[]{:S(2)}) %collective-permute-start.2) | collective-permute-done | bytes 393248 | tf_op jit(solution)/shard_map/ppermute | solution.py:30
  119.1 2.3 %collective-permute-done.3 = f32[6,128,128]{2,0,1:T(8,128)S(1)} collective-permute-done((f32[6,128,128]{2,0,1:T(8,128)S(1)}, f32[6,128,128]{2,0,1:T(8,128)S(1)}, u32[]{:S(2)}, u32[]{:S(2)}) %collective-permute-start.3) | collective-permute-done | bytes 393248 | tf_op jit(solution)/shard_map/ppermute | solution.py:33
  121.4 0.8 copy-done.4
  122.2 10.2 %fusion.65 = f32[16,128,128]{2,0,1:T(8,128)S(1)} fusion(f32[16,128,128]{2,0,1:T(8,128)S(1)} %get-tuple-element.5, f32[16,6,128]{2,0,1:T(8,128)S(1)} %get-tuple-element.26, f32[16,6,128]{2,0,1:T(8,128)S(1)} %get-tuple-element.25, f32[6,128,128]{2,0,1:T(8,128)} %copy-done.4, f32[6,128,128]{2,0,1:T(8,128)} %copy-done.2, ...), kind=kLoop, calls=%fused_computation.164 | loop fusion | flops 19660800 | bytes 18710528 | tf_op jit(solution)/shard_map/sub | solution.py:76
  132.4 0.8 collective-permute-start.4
  133.2 1.5 collective-permute-start.5
  135.2 0.8 maximum_maximum_fusion.2
  136.0 9.7 %collective-permute-done.4 = f32[6,128,128]{2,0,1:T(8,128)S(1)} collective-permute-done((f32[6,128,128]{2,0,1:T(8,128)S(1)}, f32[6,128,128]{2,0,1:T(8,128)S(1)}, u32[]{:S(2)}, u32[]{:S(2)}) %collective-permute-start.4) | collective-permute-done | bytes 393248 | tf_op jit(solution)/shard_map/ppermute | solution.py:30
  145.7 2.6 %collective-permute-done.5 = f32[6,128,128]{2,0,1:T(8,128)S(1)} collective-permute-done((f32[6,128,128]{2,0,1:T(8,128)S(1)}, f32[6,128,128]{2,0,1:T(8,128)S(1)}, u32[]{:S(2)}, u32[]{:S(2)}) %collective-permute-start.5) | collective-permute-done | bytes 393248 | tf_op jit(solution)/shard_map/ppermute | solution.py:33
  148.3 0.8 copy-done.3
  149.1 7.7 %fusion.14 = f32[1,16,128,128]{3,1,2,0:T(8,128)S(1)} fusion(f32[16,128,128]{2,0,1:T(8,128)S(1)} %fusion.65, f32[16,6,128]{2,0,1:T(8,128)S(1)} %get-tuple-element.22, f32[16,6,128]{2,0,1:T(8,128)S(1)} %get-tuple-element.21, f32[6,128,128]{2,0,1:T(8,128)} %copy-done.3, f32[6,128,128]{2,0,1:T(8,128)S(1)} %collective-permute-done.4, ...), kind=kLoop, calls=%fused_computation.113 | loop fusion | flops 19660800 | bytes 17661952 | tf_op jit(solution)/shard_map/broadcast_in_dim | solution.py:79
  156.8 1.3 copy.7
  (22 shorter events, 1.6 us)
Async XLA Ops:
  6.5 83.8 %all-gather.2.cloned.1.call-start = ((), (), s32[]{:S(2)}) async-start(), calls=%async_computation | async-start | bytes 1081344 | tf_op jit(solution)/shard_map/all_gather | solution.py:66
  9.9 13.8 %collective-permute-start = (f32[6,128,128]{2,0,1:T(8,128)S(1)}, f32[6,128,128]{2,0,1:T(8,128)}, u32[]{:S(2)}, u32[]{:S(2)}) collective-permute-start(f32[6,128,128]{2,0,1:T(8,128)S(1)} %get-tuple-element.27), channel_id=1, source_target_pairs={{0,1},{1,2},{2,3},{3,4},{4,5},{5,6},{6,7},{7,0},{8,9},{9,10},{10,1... | collective-permute-start | bytes 1179656 | tf_op jit(solution)/shard_map/ppermute | solution.py:30
  11.1 15.6 %collective-permute-start.1 = (f32[6,128,128]{2,0,1:T(8,128)S(1)}, f32[6,128,128]{2,0,1:T(8,128)}, u32[]{:S(2)}, u32[]{:S(2)}) collective-permute-start(f32[6,128,128]{2,0,1:T(8,128)S(1)} %get-tuple-element.28), channel_id=1, source_target_pairs={{1,0},{2,1},{3,2},{4,3},{5,4},{6,5},{7,6},{0,7},{9,8},{10,9},{11,1... | collective-permute-start | bytes 1179656 | tf_op jit(solution)/shard_map/ppermute | solution.py:33
  104.9 14.2 %collective-permute-start.2 = (f32[6,128,128]{2,0,1:T(8,128)S(1)}, f32[6,128,128]{2,0,1:T(8,128)S(1)}, u32[]{:S(2)}, u32[]{:S(2)}) collective-permute-start(f32[6,128,128]{2,0,1:T(8,128)S(1)} %get-tuple-element.23), channel_id=1, source_target_pairs={{0,1},{1,2},{2,3},{3,4},{4,5},{5,6},{6,7},{7,0},{8,9},{9,10},{10,1... | collective-permute-start | bytes 1179656 | tf_op jit(solution)/shard_map/ppermute | solution.py:30
  105.4 15.9 %collective-permute-start.3 = (f32[6,128,128]{2,0,1:T(8,128)S(1)}, f32[6,128,128]{2,0,1:T(8,128)S(1)}, u32[]{:S(2)}, u32[]{:S(2)}) collective-permute-start(f32[6,128,128]{2,0,1:T(8,128)S(1)} %get-tuple-element.24), channel_id=1, source_target_pairs={{1,0},{2,1},{3,2},{4,3},{5,4},{6,5},{7,6},{0,7},{9,8},{10,9},{11,1... | collective-permute-start | bytes 1179656 | tf_op jit(solution)/shard_map/ppermute | solution.py:33
  107.4 14.7 %copy-start = (f32[16,128,128]{2,0,1:T(8,128)S(1)}, f32[16,128,128]{2,0,1:T(8,128)}, u32[]{:S(2)}) copy-start(f32[16,128,128]{2,0,1:T(8,128)} %all-gather.2.cloned.1.call-done) | copy-start | bytes 3145732
  119.1 2.3 %copy-start.2 = (f32[6,128,128]{2,0,1:T(8,128)}, f32[6,128,128]{2,0,1:T(8,128)S(1)}, u32[]{:S(2)}) copy-start(f32[6,128,128]{2,0,1:T(8,128)S(1)} %collective-permute-done.2) | copy-start | bytes 1179652
  121.4 0.8 copy-start.4
  132.4 13.2 %collective-permute-start.4 = (f32[6,128,128]{2,0,1:T(8,128)S(1)}, f32[6,128,128]{2,0,1:T(8,128)S(1)}, u32[]{:S(2)}, u32[]{:S(2)}) collective-permute-start(f32[6,128,128]{2,0,1:T(8,128)S(1)} %get-tuple-element.19), channel_id=1, source_target_pairs={{0,1},{1,2},{2,3},{3,4},{4,5},{5,6},{6,7},{7,0},{8,9},{9,10},{10,1... | collective-permute-start | bytes 1179656 | tf_op jit(solution)/shard_map/ppermute | solution.py:30
  133.2 15.1 %collective-permute-start.5 = (f32[6,128,128]{2,0,1:T(8,128)S(1)}, f32[6,128,128]{2,0,1:T(8,128)S(1)}, u32[]{:S(2)}, u32[]{:S(2)}) collective-permute-start(f32[6,128,128]{2,0,1:T(8,128)S(1)} %get-tuple-element.20), channel_id=1, source_target_pairs={{1,0},{2,1},{3,2},{4,3},{5,4},{6,5},{7,6},{0,7},{9,8},{10,9},{11,1... | collective-permute-start | bytes 1179656 | tf_op jit(solution)/shard_map/ppermute | solution.py:33
  135.2 13.9 %copy-start.1 = (f32[16,128,128]{2,0,1:T(8,128)S(1)}, f32[16,128,128]{2,0,1:T(8,128)}, u32[]{:S(2)}) copy-start(f32[16,128,128]{2,0,1:T(8,128)} %get-tuple-element.6) | copy-start | bytes 3145732
  148.3 0.8 copy-start.3
Sparse Core Ops, SparseCore 0:
  10.1 80.1 all-gather.1
where the time goes:
time: 165 us
  waiting for transfers between devices  101 us (61%)
  other arithmetic  36.4 us (22%)
  between operations  13.5 us (8%)
  local copies, waits for them, and re-layouts  7.44 us (5%)
  starting transfers between devices  6.49 us (4%)
    all_gather x1, waiting for transfers between devices, shards(): vfull = lax.all_gather(potential, 'band', axis=1, tiled=True)  63.7 us
    ppermute x3, waiting for transfers between devices, with_halo(): lax.ppermute(lax.slice_in_dim(block, block.shape[dim] - width, None, axis...  29.5 us
    mul x1, other arithmetic, shards(): sigma_one / UPPER_HALF  14.4 us
    sub x1, other arithmetic, shards(): 2.0 * tnext / UPPER_HALF * (image - CENTER * newer) - sigma * tnext * older  10.2 us
    ppermute x3, waiting for transfers between devices, with_halo(): lax.ppermute(lax.slice_in_dim(block, 0, width, axis=dim), axis, backward)  7.92 us
    broadcast_in_dim x1, other arithmetic, shards(): return newer[None]  7.7 us
    unnamed x12, local copies, waits for them, and re-layouts  4.82 us
    concatenate x6, other arithmetic, hamil_padded(): wrapped = jnp.pad(center, ((0, 0), (6, 6), (6, 6)), mode='wrap')  4.07 us
  transfers between devices with their start and end apart: 7, of which 7 were waited for; matrix products, arithmetic and copies ran while one was open for 4% of the time, Pallas kernels for 0%

commit v1 on v0

v1 whole, which is shorter than its diff:
```python
import functools

import jax
import jax.numpy as jnp
import ml_dtypes
import numpy as np
from jax import lax
from jax.experimental import pallas as pl
from jax.experimental.pallas import tpu as pltpu
from jax.sharding import PartitionSpec as P

DEGREE = 3
COEFS = (
    -5369.0 / 1800.0,
    12.0 / 7.0,
    -15.0 / 56.0,
    10.0 / 189.0,
    -1.0 / 112.0,
    2.0 / 1925.0,
    -1.0 / 16632.0,
)
INVERSE_SQ = 1.0 / 0.64
UPPER_HALF = 10.0
CENTER = 10.0
FLOOR = -5.0

KIN = tuple(-0.5 * INVERSE_SQ * c for c in COEFS)
SIGMA1 = UPPER_HALF / (FLOOR - CENTER)
GAMMA = 2.0 / SIGMA1
SIGMA2 = 1.0 / (GAMMA - SIGMA1)
SIGMA3 = 1.0 / (GAMMA - SIGMA2)
STEP1 = (SIGMA1 / UPPER_HALF, None)
STEP2 = (2.0 * SIGMA2 / UPPER_HALF, SIGMA1 * SIGMA2)
STEP3 = (2.0 * SIGMA3 / UPPER_HALF, SIGMA2 * SIGMA3)

W = 6
F32 = jnp.float32
BF16 = jnp.bfloat16
SLOTS_S = ((0, 0), (0, 1), (3, 0), (3, 1), (-3, 0), (-3, 1))
SLOTS_U = tuple((dz + 1, dh) for dz, dh in SLOTS_S)
SLOTS_D = tuple((dz - 1, dh) for dz, dh in SLOTS_S[:4])
SLOTS = SLOTS_S + SLOTS_U + SLOTS_D


def circulant(n):
    dense = np.zeros((n, n), np.float64)
    for k in range(1, W + 1):
        for i in range(n):
            dense[i, (i + k) % n] += KIN[k]
            dense[i, (i - k) % n] += KIN[k]
    high = dense.astype(ml_dtypes.bfloat16)
    low = (dense - high.astype(np.float64)).astype(ml_dtypes.bfloat16)
    return np.block([[high, low], [high, low]])


def in_planes(planes, left, right, out):
    n = left.shape[0] // 2
    for i in range(0, len(planes), 2):
        pair = [planes[i][...], planes[i + 1][...]]
        high = [f.astype(BF16) for f in pair]
        low = [(f - h.astype(F32)).astype(BF16) for f, h in zip(pair, high)]
        tall = jnp.concatenate([jnp.concatenate(high, 1), jnp.concatenate(low, 1)], 0)
        wide = jnp.concatenate([jnp.concatenate(high, 0), jnp.concatenate(low, 0)], 1)
        along_y = jnp.dot(left[...], tall, preferred_element_type=F32)
        along_z = jnp.dot(wide, right[...], preferred_element_type=F32)
        along_y = along_y[:n] + along_y[n:]
        along_z = along_z[:, :n] + along_z[:, n:]
        out[i] = along_y[:, :n] + along_z[:n]
        out[i + 1] = along_y[:, n:] + along_z[n:]


def over_tiles(n, body):
    def step(t, carry):
        body(pl.ds(pl.multiple_of(t * 8, 8), 8))
        return carry

    lax.fori_loop(0, n // 8, step, 0)


def along_x(vals, at, scale, total):
    for k in range(1, W + 1):
        below, above = vals.get(at - k), vals.get(at + k)
        if below is None and above is None:
            continue
        near = above if below is None else (below if above is None else below + above)
        total = total + (scale * KIN[k]) * near
    return total


def place_potential(own_refs, other_refs, slots_of, planes, out):
    me = lax.axis_index("band")
    z, h, c = me // 4, (me // 2) % 2, me % 2
    mine_first = c == 0
    for own, other, slots in zip(own_refs, other_refs, slots_of):
        for i, (dz, dh) in enumerate(slots):
            zz = lax.rem(z + (dz + 8), 8)
            hh = (h + dh) % 2
            rows = pl.ds(pl.multiple_of(zz * 16 + hh * 8, 8), 8)
            for q in range(planes // 2):
                a = own[i, 8 * q : 8 * q + 8, :]
                b = other[i, 8 * q : 8 * q + 8, :]
                first = jnp.where(mine_first, a, b)
                second = jnp.where(mine_first, b, a)
                out[2 * q, rows, :] = jnp.concatenate([first[:4], second[:4]], 0)
                out[2 * q + 1, rows, :] = jnp.concatenate([first[4:], second[4:]], 0)


def kernel_own(x, left, right, w1, flat):
    in_planes([x.at[p] for p in range(16)], left, right, flat)

    def body(rows):
        vals = {p: x[p, rows, :] for p in range(16)}
        for p in range(16):
            total = flat[p, rows, :] + (3.0 * KIN[0] - CENTER) * vals[p]
            w1[p, rows, :] = along_x(vals, p, 1.0, total)

    over_tiles(x.shape[1], body)


def kernel_first(x, w1, xl, xr, s0, u0, d0, s1, u1, d1, y1, to_left, to_right, vown):
    place_potential((s0, u0, d0), (s1, u1, d1), (SLOTS_S, SLOTS_U, SLOTS_D), 16, vown)
    alpha = STEP1[0]

    def body(rows):
        vals = {p - 12: xl[p, rows, :] for p in range(6, 12)}
        vals.update({p + 16: xr[p, rows, :] for p in range(6)})
        for p in range(16):
            total = w1[p, rows, :] + vown[p, rows, :] * x[p, rows, :]
            value = alpha * along_x(vals, p, 1.0, total)
            y1[p, rows, :] = value
            if 6 <= p < 12:
                to_left[p - 6, rows, :] = value
            if 4 <= p < 10:
                to_right[p - 4, rows, :] = value

    over_tiles(x.shape[1], body)


def kernel_middle(
    x, xl, xr, y1, left, right, vown, hl0, hr0, hl1, hr1, y2l, y2r, y3, y1l, y1r, y2, vl, vr, flat
):
    n = x.shape[1]
    place_potential((hl0,), (hl1,), (SLOTS,), W, vl)
    place_potential((hr0,), (hr1,), (SLOTS,), W, vr)

    def x_at(p, rows):
        return xl[p + 12, rows, :] if p < 0 else (x[p, rows, :] if p < 16 else xr[p - 16, rows, :])

    def y1_at(p, rows):
        return y1l[p + 6, rows, :] if p < 0 else (y1[p, rows, :] if p < 16 else y1r[p - 16, rows, :])

    sides = ((-6, y1l, vl, y2l), (16, y1r, vr, y2r))
    in_planes([xl.at[p + 6] for p in range(6)] + [xr.at[p] for p in range(6)], left, right, flat)

    def first_sides(rows):
        for s, (start, dest, pot, _) in enumerate(sides):
            vals = {p: x_at(p, rows) for p in range(start - 6, start + 12)}
            for j in range(6):
                mid = vals[start + j]
                total = flat[6 * s + j, rows, :] + (pot[j, rows, :] + (3.0 * KIN[0] - CENTER)) * mid
                dest[j, rows, :] = STEP1[0] * along_x(vals, start + j, 1.0, total)

    over_tiles(n, first_sides)

    alpha, beta = STEP2
    in_planes([y1.at[p] for p in range(16)], left, right, flat)

    def second(rows):
        vals = {p: y1_at(p, rows) for p in range(-6, 22)}
        for p in range(16):
            total = flat[p, rows, :] + (vown[p, rows, :] + (3.0 * KIN[0] - CENTER)) * vals[p]
            y2[p, rows, :] = alpha * along_x(vals, p, 1.0, total) - beta * x[p, rows, :]

    over_tiles(n, second)
    in_planes([y1l.at[p] for p in range(6)] + [y1r.at[p] for p in range(6)], left, right, flat)

    def second_sides(rows):
        for s, (start, source, pot, dest) in enumerate(sides):
            low = max(start - 6, -6)
            vals = {p: y1_at(p, rows) for p in range(low, min(start + 12, 22))}
            for j in range(6):
                total = flat[6 * s + j, rows, :] + (pot[j, rows, :] + (3.0 * KIN[0] - CENTER)) * vals[start + j]
                dest[j, rows, :] = alpha * along_x(vals, start + j, 1.0, total) - beta * x_at(start + j, rows)

    over_tiles(n, second_sides)
    alpha3, beta3 = STEP3
    in_planes([y2.at[p] for p in range(16)], left, right, flat)

    def third(rows):
        vals = {p: y2[p, rows, :] for p in range(16)}
        for p in range(16):
            total = flat[p, rows, :] + (vown[p, rows, :] + (3.0 * KIN[0] - CENTER)) * vals[p]
            y3[p, rows, :] = alpha3 * along_x(vals, p, 1.0, total) - beta3 * y1[p, rows, :]

    over_tiles(n, third)


def kernel_last(far_l, far_r, y2l, y2r, y3, out):
    def body(rows):
        far = {p - 12: far_l[p, rows, :] for p in range(6)}
        far.update({p + 22: far_r[p, rows, :] for p in range(6)})
        near = {}
        for j in range(6):
            near[j - 6] = along_x(far, j - 6, STEP2[0], y2l[j, rows, :])
            near[j + 16] = along_x(far, j + 16, STEP2[0], y2r[j, rows, :])
        for p in range(16):
            out[p, rows, :] = along_x(near, p, STEP3[0], y3[p, rows, :])

    over_tiles(out.shape[1], body)


def call(body, outs, scratch, args, flops):
    whole = pl.BlockSpec(memory_space=pltpu.VMEM)
    total = sum(a.size * a.dtype.itemsize for a in args) + sum(4 * int(np.prod(o)) for o in outs)
    return pl.pallas_call(
        body,
        out_shape=tuple(jax.ShapeDtypeStruct(o, F32) for o in outs),
        in_specs=[whole] * len(args),
        out_specs=tuple(whole for _ in outs),
        scratch_shapes=[pltpu.VMEM(s, F32) for s in scratch],
        compiler_params=pltpu.CompilerParams(vmem_limit_bytes=40 * 1024 * 1024),
        cost_estimate=pl.CostEstimate(flops=flops, bytes_accessed=total, transcendentals=0),
    )(*args)


def shards(orbital, potential):
    x = orbital[0]
    nx, ny, nz = x.shape
    bands, slabs = lax.axis_size("band"), lax.axis_size("slab")
    up = [(i, (i + 1) % slabs) for i in range(slabs)]
    down = [(b, a) for a, b in up]

    def from_z(value, d):
        return lax.ppermute(value, "band", [((i + 4 * d) % bands, i) for i in range(bands)])

    def flip(value, bit):
        return lax.ppermute(value, "band", [(i ^ bit, i) for i in range(bands)])

    plane = (ny, nz)
    block = potential.reshape(1, nx * potential.shape[1], nz)
    last, first, block = lax.optimization_barrier((x[nx - 12 :], x[:12], block))
    xl = lax.ppermute(last, "slab", up)
    xr = lax.ppermute(first, "slab", down)

    s0 = jnp.concatenate([block, flip(block, 2)], 0)
    s0 = jnp.concatenate([s0, from_z(s0, 3), from_z(s0, -3)], 0)
    u0, d0 = from_z(s0, 1), from_z(s0[:4], -1)
    s1, u1, d1 = flip(s0, 1), flip(u0, 1), flip(d0, 1)
    gathered = (s0, u0, d0)
    hl0 = lax.ppermute(jnp.concatenate([g[:, 40:] for g in gathered], 0), "slab", up)
    hr0 = lax.ppermute(jnp.concatenate([g[:, :24] for g in gathered], 0), "slab", down)
    hl1, hr1 = flip(hl0, 1), flip(hr0, 1)

    mat = circulant(ny)
    right = jnp.asarray(mat)
    left = jnp.asarray(np.ascontiguousarray(mat.T))
    cells = nx * ny * nz
    six, own = (6, *plane), (16, *plane)
    (w1,) = call(kernel_own, [own], [own], [x, left, right], 40 * cells)
    y1, to_left, to_right, vown = call(
        kernel_first, [own, six, six, own], [], [x, w1, xl, xr, s0, u0, d0, s1, u1, d1], 10 * cells
    )
    far_r = lax.ppermute(to_left, "slab", down)
    far_l = lax.ppermute(to_right, "slab", up)
    y2l, y2r, y3 = call(
        kernel_middle,
        [six, six, own],
        [six, six, own, six, six, own],
        [x, xl, xr, y1, left, right, vown, hl0, hr0, hl1, hr1],
        140 * cells,
    )
    (out,) = call(kernel_last, [own], [], [far_l, far_r, y2l, y2r, y3], 10 * cells)
    return out[None]


def solution(mesh):
    placed = (P("band", "slab", None, None), P("slab", "band", None))
    return jax.shard_map(
        shards, mesh=mesh, in_specs=placed, out_specs=P("band", "slab", None, None), check_vma=False
    )
```

time: 165 us -> 56 us (0.34)
  waiting for transfers between devices: 101 us -> 22.2 us
  other arithmetic: 36.4 us -> 0.04 us
  starting transfers between devices: 6.49 us -> 22.1 us
  between operations: 13.5 us -> 0.19 us
  Pallas kernels: 0 us -> 9.81 us
  local copies, waits for them, and re-layouts: 7.44 us -> 1.59 us
    all_gather x1 -> x0, waiting for transfers between devices: 63.7 us -> none  [shards(): vfull = lax.all_gather(potential, 'band', axis=1, tiled=True)]
    ppermute x6 -> x16, starting transfers between devices: 6.49 us -> 22.1 us  [the longest x4 8.74 us: from_z(): lax.ppermute(value, 'band', [((i + 4 * d) % bands, i) for i in range(band...]
    ppermute x6 -> x16, waiting for transfers between devices: 37.4 us -> 22.2 us  [the longest x4 13.4 us: from_z(): lax.ppermute(value, 'band', [((i + 4 * d) % bands, i) for i in range(band...]
    mul x1 -> x0, other arithmetic: 14.4 us -> none  [shards(): sigma_one / UPPER_HALF]
    sub x1 -> x0, other arithmetic: 10.2 us -> none  [shards(): 2.0 * tnext / UPPER_HALF * (image - CENTER * newer) - sigma * tnext * older]
    pallas_call x0 -> x4, Pallas kernels: none -> 9.81 us  [call(): pl.pallas_call(body, out_shape=tuple((jax.ShapeDtypeStruct(o, F32) for o...]
    broadcast_in_dim x1 -> x0, other arithmetic: 7.7 us -> none  [shards(): return newer[None]]
    unnamed x12 -> x10, local copies, waits for them, and re-layouts: 4.82 us -> 0.03 us
  transfers between devices with their start and end apart: 7 -> 16, of which waited for: 7 -> 7; matrix products, arithmetic and copies ran while one was open for 4% -> 0% of each run, Pallas kernels for 0% -> 15%
where the time goes in v1:
time: 56 us; the launch traced here: 55.9 us
  waiting for transfers between devices  22.2 us (40%)
  starting transfers between devices  22.1 us (39%)
  Pallas kernels  9.81 us (18%)
  local copies, waits for them, and re-layouts  1.59 us (3%)
    ppermute x4, waiting for transfers between devices, from_z(): lax.ppermute(value, 'band', [((i + 4 * d) % bands, i) for i in range(band...  13.4 us
    pallas_call x4, Pallas kernels, call(): pl.pallas_call(body, out_shape=tuple((jax.ShapeDtypeStruct(o, F32) for o...  9.81 us
    ppermute x4, starting transfers between devices, from_z(): lax.ppermute(value, 'band', [((i + 4 * d) % bands, i) for i in range(band...  8.74 us
    ppermute x1, starting transfers between devices, shards(): far_l = lax.ppermute(to_right, 'slab', up)  4.19 us
    ppermute x6, waiting for transfers between devices, flip(): return lax.ppermute(value, 'band', [(i ^ bit, i) for i in range(bands)])  3.84 us
    ppermute x6, starting transfers between devices, flip(): return lax.ppermute(value, 'band', [(i ^ bit, i) for i in range(bands)])  3.8 us
    ppermute x1, starting transfers between devices, shards(): lax.ppermute(jnp.concatenate([g[:, 40:] for g in gathered], 0), 'slab', up)  3.34 us
    ppermute x1, waiting for transfers between devices, shards(): far_r = lax.ppermute(to_left, 'slab', down)  2.84 us
  transfers between devices with their start and end apart: 16, of which 7 were waited for; matrix products, arithmetic and copies ran while one was open for 0% of the time, Pallas kernels for 15%

profile of v1, /device:TPU:24, one launch (start us, length us, event | category | flops | bytes accessed | tf_op | source)
XLA Modules:
  0.0 55.9 jit_solution(2910776907665251997)
XLA Ops:
  0.0 1.5 %slice_bitcast_fusion = (f32[12,128,128]{2,1,0:T(8,128)S(1)}, f32[12,128,128]{2,1,0:T(8,128)S(1)}) fusion(f32[1,16,128,128]{3,2,1,0:T(8,128)} %param.4), kind=kLoop, calls=%fused_computation | loop fusion | bytes 3145728 | tf_op jit(solution)/shard_map/slice | solution.py:241
  1.5 3.1 %collective-permute-start.2 = (f32[1,64,128]{2,1,0:T(8,128)S(1)}, f32[1,64,128]{2,1,0:T(8,128)S(1)}, u32[]{:S(2)}, u32[]{:S(2)}) collective-permute-start(f32[1,64,128]{2,1,0:T(8,128)S(1)} %bitcast.10), channel_id=1, source_target_pairs={{16,0},{24,8},{0,16},{8,24},{48,32},{56,40},{32,48},{40,56},{80,64... | collective-permute-start | bytes 98312 | tf_op jit(solution)/shard_map/ppermute | solution.py:237
  4.7 2.4 %collective-permute-done.2 = f32[1,64,128]{2,1,0:T(8,128)S(1)} collective-permute-done((f32[1,64,128]{2,1,0:T(8,128)S(1)}, f32[1,64,128]{2,1,0:T(8,128)S(1)}, u32[]{:S(2)}, u32[]{:S(2)}) %collective-permute-start.2) | collective-permute-done | bytes 32800 | tf_op jit(solution)/shard_map/ppermute | solution.py:237
  7.1 6.7 %collective-permute-start.3 = (f32[2,64,128]{2,1,0:T(8,128)S(1)}, f32[2,64,128]{2,1,0:T(8,128)S(1)}, u32[]{:S(2)}, u32[]{:S(2)}) collective-permute-start(f32[2,64,128]{2,1,0:T(8,128)S(1)} %get-tuple-element.33), channel_id=1, source_target_pairs={{96,0},{104,8},{112,16},{120,24},{128,32},{136,40},{144,48},{152,5... | collective-permute-start | bytes 196616 | tf_op jit(solution)/shard_map/ppermute | solution.py:234
  13.8 1.1 %collective-permute-start = (f32[12,128,128]{2,1,0:T(8,128)S(1)}, f32[12,128,128]{2,1,0:T(8,128)S(1)}, u32[]{:S(2)}, u32[]{:S(2)}) collective-permute-start(f32[12,128,128]{2,1,0:T(8,128)S(1)} %get-tuple-element.15), channel_id=1, source_target_pairs={{0,1},{1,2},{2,3},{3,4},{4,5},{5,6},{6,7},{7,0},{8,9},{9,10},{10,1... | collective-permute-start | bytes 2359304 | tf_op jit(solution)/shard_map/ppermute | solution.py:242
  14.9 0.9 %collective-permute-start.1 = (f32[12,128,128]{2,1,0:T(8,128)S(1)}, f32[12,128,128]{2,1,0:T(8,128)S(1)}, u32[]{:S(2)}, u32[]{:S(2)}) collective-permute-start(f32[12,128,128]{2,1,0:T(8,128)S(1)} %get-tuple-element.16), channel_id=1, source_target_pairs={{1,0},{2,1},{3,2},{4,3},{5,4},{6,5},{7,6},{0,7},{9,8},{10,9},{11,1... | collective-permute-start | bytes 2359304 | tf_op jit(solution)/shard_map/ppermute | solution.py:243
  15.8 0.7 %collective-permute-done.3 = f32[2,64,128]{2,1,0:T(8,128)S(1)} collective-permute-done((f32[2,64,128]{2,1,0:T(8,128)S(1)}, f32[2,64,128]{2,1,0:T(8,128)S(1)}, u32[]{:S(2)}, u32[]{:S(2)}) %collective-permute-start.3) | collective-permute-done | bytes 65568 | tf_op jit(solution)/shard_map/ppermute | solution.py:234
  16.5 7.6 %collective-permute-done.4 = f32[2,64,128]{2,1,0:T(8,128)S(1)} collective-permute-done((f32[2,64,128]{2,1,0:T(8,128)S(1)}, f32[2,64,128]{2,1,0:T(8,128)S(1)}, u32[]{:S(2)}, u32[]{:S(2)}) %collective-permute-start.4) | collective-permute-done | bytes 65568 | tf_op jit(solution)/shard_map/ppermute | solution.py:234
  24.1 0.1 collective-permute-start.7
  24.2 2.0 %collective-permute-start.6 = (f32[4,64,128]{2,1,0:T(8,128)S(1)}, f32[4,64,128]{2,1,0:T(8,128)S(1)}, u32[]{:S(2)}, u32[]{:S(2)}) collective-permute-start(f32[4,64,128]{2,1,0:T(8,128)S(1)} %pad_maximum_fusion.2), channel_id=1, source_target_pairs={{224,0},{232,8},{240,16},{248,24},{0,32},{8,40},{16,48},{24,56},{3... | collective-permute-start | bytes 393224 | tf_op jit(solution)/shard_map/ppermute | solution.py:234
  26.2 5.2 %collective-permute-done.6.d0 = f32[4,64,128]{2,1,0:T(8,128)S(1)} collective-permute-done((f32[4,64,128]{2,1,0:T(8,128)S(1)}, f32[4,64,128]{2,1,0:T(8,128)S(1)}, u32[]{:S(2)}, u32[]{:S(2)}) %collective-permute-start.6) | collective-permute-done | bytes 131104 | tf_op jit(solution)/shard_map/ppermute | solution.py:234
  31.4 0.6 %collective-permute-start.8 = (f32[6,64,128]{2,1,0:T(8,128)S(1)}, f32[6,64,128]{2,1,0:T(8,128)S(1)}, u32[]{:S(2)}, u32[]{:S(2)}) collective-permute-start(f32[6,64,128]{2,1,0:T(8,128)S(1)} %collective-permute-done.5.u0), channel_id=1, source_target_pairs={{8,0},{0,8},{24,16},{16,24},{40,32},{32,40},{56,48},{48,56},{72,64... | collective-permute-start | bytes 589832 | tf_op jit(solution)/shard_map/ppermute | solution.py:237
  32.1 0.0 copy-start.1
  32.1 0.0 copy-start.2
  32.1 3.3 %collective-permute-start.12 = (f32[16,24,128]{2,1,0:T(8,128)S(1)}, f32[16,24,128]{2,1,0:T(8,128)S(1)}, u32[]{:S(2)}, u32[]{:S(2)}) collective-permute-start(f32[16,24,128]{2,1,0:T(8,128)S(1)} %pad_maximum_fusion), channel_id=1, source_target_pairs={{0,1},{1,2},{2,3},{3,4},{4,5},{5,6},{6,7},{7,0},{8,9},{9,10},{10,1... | collective-permute-start | bytes 589832 | tf_op jit(solution)/shard_map/ppermute | solution.py:250
  35.5 1.4 %shard_map.46.w1 = f32[16,128,128]{2,1,0:T(8,128)S(1)} custom-call(f32[16,128,128]{2,1,0:T(8,128)S(1)} %bitcast.7, bf16[256,256]{1,0:T(8,128)(2,1)S(1)} %copy-done.1, bf16[256,256]{1,0:T(8,128)(2,1)S(1)} %copy-done.2), custom_call_target="tpu_custom_call" | custom-call | flops 10485760 | bytes 2359296 | tf_op jit(solution)/shard_map/pallas_call | solution.py:215
  36.9 0.9 %shard_map.47 = (f32[16,128,128]{2,1,0:T(8,128)S(1)}, f32[6,128,128]{2,1,0:T(8,128)S(1)}, f32[6,128,128]{2,1,0:T(8,128)S(1)}, f32[16,128,128]{2,1,0:T(8,128)S(1)}) custom-call(f32[16,128,128]{2,1,0:T(8,128)S(1)} %bitcast.8, f32[16,128,128]{2,1,0:T(8,128)S(1)} %shard_map.46.w1, f32[12,128,128]{2,1,0:T(8,128)S(1)} %collective-permute-done.xl, ...), custom_call_target="tpu_custom_call" | custom-call | flops 2621440 | bytes 7602176 | tf_op jit(solution)/shard_map/pallas_call | solution.py:215
  37.9 4.2 %collective-permute-start.10 = (f32[6,128,128]{2,1,0:T(8,128)S(1)}, f32[6,128,128]{2,1,0:T(8,128)S(1)}, u32[]{:S(2)}, u32[]{:S(2)}) collective-permute-start(f32[6,128,128]{2,1,0:T(8,128)S(1)} %get-tuple-element.18), channel_id=1, source_target_pairs={{0,1},{1,2},{2,3},{3,4},{4,5},{5,6},{6,7},{7,0},{8,9},{9,10},{10,1... | collective-permute-start | bytes 1179656 | tf_op jit(solution)/shard_map/ppermute | solution.py:264
  42.1 2.0 %collective-permute-done.13.hr0 = f32[16,24,128]{2,1,0:T(8,128)S(1)} collective-permute-done((f32[16,24,128]{2,1,0:T(8,128)S(1)}, f32[16,24,128]{2,1,0:T(8,128)S(1)}, u32[]{:S(2)}, u32[]{:S(2)}) %collective-permute-start.13) | collective-permute-done | bytes 196640 | tf_op jit(solution)/shard_map/ppermute | solution.py:251
  44.1 0.0 collective-permute-start.15
  44.1 1.4 %collective-permute-done.15.hr1 = f32[16,24,128]{2,1,0:T(8,128)S(1)} collective-permute-done((f32[16,24,128]{2,1,0:T(8,128)S(1)}, f32[16,24,128]{2,1,0:T(8,128)S(1)}, u32[]{:S(2)}, u32[]{:S(2)}) %collective-permute-start.15) | collective-permute-done | bytes 196640 | tf_op jit(solution)/shard_map/ppermute | solution.py:237
  45.6 6.0 %shard_map.48 = (f32[6,128,128]{2,1,0:T(8,128)S(1)}, f32[6,128,128]{2,1,0:T(8,128)S(1)}, f32[16,128,128]{2,1,0:T(8,128)S(1)}) custom-call(f32[16,128,128]{2,1,0:T(8,128)S(1)} %bitcast.9, f32[12,128,128]{2,1,0:T(8,128)S(1)} %collective-permute-done.xl, f32[12,128,128]{2,1,0:T(8,128)S(1)} %collective-permute-done.1.xr, ...), custom_call_target="tpu_custom_call" | custom-call | flops 36700160 | bytes 7602176 | tf_op jit(solution)/shard_map/pallas_call | solution.py:215
  51.5 2.8 %collective-permute-done.11.far_r = f32[6,128,128]{2,1,0:T(8,128)S(1)} collective-permute-done((f32[6,128,128]{2,1,0:T(8,128)S(1)}, f32[6,128,128]{2,1,0:T(8,128)S(1)}, u32[]{:S(2)}, u32[]{:S(2)}) %collective-permute-start.11) | collective-permute-done | bytes 393248 | tf_op jit(solution)/shard_map/ppermute | solution.py:263
  54.4 1.5 %shard_map.49 = f32[16,128,128]{2,1,0:T(8,128)} custom-call(f32[6,128,128]{2,1,0:T(8,128)S(1)} %collective-permute-done.10.far_l, f32[6,128,128]{2,1,0:T(8,128)S(1)} %collective-permute-done.11.far_r, f32[6,128,128]{2,1,0:T(8,128)S(1)} %get-tuple-element.22.y2l, f32[6,128,128]{2,1,0:T(8,128)S(1)} %get-tuple-element.23.y2r, ...), custom_call_target="tpu_custom_call" | custom-call | flops 2621440 | bytes 3670016 | tf_op jit(solution)/shard_map/pallas_call | solution.py:215
  (31 shorter events, 0.1 us)
Async XLA Ops:
  0.0 1.5 %copy-start.3 = (f32[16,4,128]{2,1,0:T(4,128)S(1)}, f32[16,4,128]{2,1,0:T(4,128)}, u32[]{:S(2)}) copy-start(f32[16,4,128]{2,1,0:T(4,128)} %param.5) | copy-start | bytes 98308
  1.5 5.5 %collective-permute-start.2 = (f32[1,64,128]{2,1,0:T(8,128)S(1)}, f32[1,64,128]{2,1,0:T(8,128)S(1)}, u32[]{:S(2)}, u32[]{:S(2)}) collective-permute-start(f32[1,64,128]{2,1,0:T(8,128)S(1)} %bitcast.10), channel_id=1, source_target_pairs={{16,0},{24,8},{0,16},{8,24},{48,32},{56,40},{32,48},{40,56},{80,64... | collective-permute-start | bytes 98312 | tf_op jit(solution)/shard_map/ppermute | solution.py:237
  7.1 9.4 %collective-permute-start.3 = (f32[2,64,128]{2,1,0:T(8,128)S(1)}, f32[2,64,128]{2,1,0:T(8,128)S(1)}, u32[]{:S(2)}, u32[]{:S(2)}) collective-permute-start(f32[2,64,128]{2,1,0:T(8,128)S(1)} %get-tuple-element.33), channel_id=1, source_target_pairs={{96,0},{104,8},{112,16},{120,24},{128,32},{136,40},{144,48},{152,5... | collective-permute-start | bytes 196616 | tf_op jit(solution)/shard_map/ppermute | solution.py:234
  13.8 23.1 %collective-permute-start = (f32[12,128,128]{2,1,0:T(8,128)S(1)}, f32[12,128,128]{2,1,0:T(8,128)S(1)}, u32[]{:S(2)}, u32[]{:S(2)}) collective-permute-start(f32[12,128,128]{2,1,0:T(8,128)S(1)} %get-tuple-element.15), channel_id=1, source_target_pairs={{0,1},{1,2},{2,3},{3,4},{4,5},{5,6},{6,7},{7,0},{8,9},{9,10},{10,1... | collective-permute-start | bytes 2359304 | tf_op jit(solution)/shard_map/ppermute | solution.py:242
  14.9 22.0 %collective-permute-start.1 = (f32[12,128,128]{2,1,0:T(8,128)S(1)}, f32[12,128,128]{2,1,0:T(8,128)S(1)}, u32[]{:S(2)}, u32[]{:S(2)}) collective-permute-start(f32[12,128,128]{2,1,0:T(8,128)S(1)} %get-tuple-element.16), channel_id=1, source_target_pairs={{1,0},{2,1},{3,2},{4,3},{5,4},{6,5},{7,6},{0,7},{9,8},{10,9},{11,1... | collective-permute-start | bytes 2359304 | tf_op jit(solution)/shard_map/ppermute | solution.py:243
  15.8 8.3 %collective-permute-start.4 = (f32[2,64,128]{2,1,0:T(8,128)S(1)}, f32[2,64,128]{2,1,0:T(8,128)S(1)}, u32[]{:S(2)}, u32[]{:S(2)}) collective-permute-start(f32[2,64,128]{2,1,0:T(8,128)S(1)} %get-tuple-element.33), channel_id=1, source_target_pairs={{160,0},{168,8},{176,16},{184,24},{192,32},{200,40},{208,48},{216,... | collective-permute-start | bytes 196616 | tf_op jit(solution)/shard_map/ppermute | solution.py:234
  16.5 19.0 %copy-start = (f32[1,16,128,128]{3,2,1,0:T(8,128)S(1)}, f32[1,16,128,128]{3,2,1,0:T(8,128)}, u32[]{:S(2)}) copy-start(f32[1,16,128,128]{3,2,1,0:T(8,128)} %param.4) | copy-start | bytes 3145732
  24.1 7.3 %collective-permute-start.5 = (f32[6,64,128]{2,1,0:T(8,128)S(1)}, f32[6,64,128]{2,1,0:T(8,128)S(1)}, u32[]{:S(2)}, u32[]{:S(2)}) collective-permute-start(f32[6,64,128]{2,1,0:T(8,128)S(1)} %constant_dynamic-update-slice_fusion.2.s0), channel_id=1, source_target_pairs={{32,0},{40,8},{48,16},{56,24},{64,32},{72,40},{80,48},{88,56},{96,... | collective-permute-start | bytes 589832 | tf_op jit(solution)/shard_map/ppermute | solution.py:234
  24.1 8.0 %collective-permute-start.7 = (f32[6,64,128]{2,1,0:T(8,128)S(1)}, f32[6,64,128]{2,1,0:T(8,128)S(1)}, u32[]{:S(2)}, u32[]{:S(2)}) collective-permute-start(f32[6,64,128]{2,1,0:T(8,128)S(1)} %constant_dynamic-update-slice_fusion.2.s0), channel_id=1, source_target_pairs={{8,0},{0,8},{24,16},{16,24},{40,32},{32,40},{56,48},{48,56},{72,64... | collective-permute-start | bytes 589832 | tf_op jit(solution)/shard_map/ppermute | solution.py:237
  24.2 7.2 %collective-permute-start.6 = (f32[4,64,128]{2,1,0:T(8,128)S(1)}, f32[4,64,128]{2,1,0:T(8,128)S(1)}, u32[]{:S(2)}, u32[]{:S(2)}) collective-permute-start(f32[4,64,128]{2,1,0:T(8,128)S(1)} %pad_maximum_fusion.2), channel_id=1, source_target_pairs={{224,0},{232,8},{240,16},{248,24},{0,32},{8,40},{16,48},{24,56},{3... | collective-permute-start | bytes 393224 | tf_op jit(solution)/shard_map/ppermute | solution.py:234
  31.4 4.0 %collective-permute-start.9 = (f32[4,64,128]{2,1,0:T(8,128)S(1)}, f32[4,64,128]{2,1,0:T(8,128)S(1)}, u32[]{:S(2)}, u32[]{:S(2)}) collective-permute-start(f32[4,64,128]{2,1,0:T(8,128)S(1)} %collective-permute-done.6.d0), channel_id=1, source_target_pairs={{8,0},{0,8},{24,16},{16,24},{40,32},{32,40},{56,48},{48,56},{72,64... | collective-permute-start | bytes 393224 | tf_op jit(solution)/shard_map/ppermute | solution.py:237
  31.4 5.5 %collective-permute-start.8 = (f32[6,64,128]{2,1,0:T(8,128)S(1)}, f32[6,64,128]{2,1,0:T(8,128)S(1)}, u32[]{:S(2)}, u32[]{:S(2)}) collective-permute-start(f32[6,64,128]{2,1,0:T(8,128)S(1)} %collective-permute-done.5.u0), channel_id=1, source_target_pairs={{8,0},{0,8},{24,16},{16,24},{40,32},{32,40},{56,48},{48,56},{72,64... | collective-permute-start | bytes 589832 | tf_op jit(solution)/shard_map/ppermute | solution.py:237
  32.1 3.4 %copy-start.1 = (bf16[256,256]{1,0:T(8,128)(2,1)S(1)}, bf16[256,256]{1,0:T(8,128)(2,1)}, u32[]{:S(2)}) copy-start(bf16[256,256]{1,0:T(8,128)(2,1)} %constant.5.clone.left) | copy-start | bytes 393220
  32.1 3.4 %copy-start.2 = (bf16[256,256]{1,0:T(8,128)(2,1)S(1)}, bf16[256,256]{1,0:T(8,128)(2,1)}, u32[]{:S(2)}) copy-start(bf16[256,256]{1,0:T(8,128)(2,1)} %constant.4.clone.right) | copy-start | bytes 393220
  32.1 10.0 %collective-permute-start.12 = (f32[16,24,128]{2,1,0:T(8,128)S(1)}, f32[16,24,128]{2,1,0:T(8,128)S(1)}, u32[]{:S(2)}, u32[]{:S(2)}) collective-permute-start(f32[16,24,128]{2,1,0:T(8,128)S(1)} %pad_maximum_fusion), channel_id=1, source_target_pairs={{0,1},{1,2},{2,3},{3,4},{4,5},{5,6},{6,7},{7,0},{8,9},{9,10},{10,1... | collective-permute-start | bytes 589832 | tf_op jit(solution)/shard_map/ppermute | solution.py:250
  35.5 8.7 %collective-permute-start.13 = (f32[16,24,128]{2,1,0:T(8,128)S(1)}, f32[16,24,128]{2,1,0:T(8,128)S(1)}, u32[]{:S(2)}, u32[]{:S(2)}) collective-permute-start(f32[16,24,128]{2,1,0:T(8,128)S(1)} %pad_maximum_fusion.1), channel_id=1, source_target_pairs={{1,0},{2,1},{3,2},{4,3},{5,4},{6,5},{7,6},{0,7},{9,8},{10,9},{11,1... | collective-permute-start | bytes 589832 | tf_op jit(solution)/shard_map/ppermute | solution.py:251
  37.9 13.7 %collective-permute-start.10 = (f32[6,128,128]{2,1,0:T(8,128)S(1)}, f32[6,128,128]{2,1,0:T(8,128)S(1)}, u32[]{:S(2)}, u32[]{:S(2)}) collective-permute-start(f32[6,128,128]{2,1,0:T(8,128)S(1)} %get-tuple-element.18), channel_id=1, source_target_pairs={{0,1},{1,2},{2,3},{3,4},{4,5},{5,6},{6,7},{7,0},{8,9},{9,10},{10,1... | collective-permute-start | bytes 1179656 | tf_op jit(solution)/shard_map/ppermute | solution.py:264
  42.1 12.3 %collective-permute-start.11 = (f32[6,128,128]{2,1,0:T(8,128)S(1)}, f32[6,128,128]{2,1,0:T(8,128)S(1)}, u32[]{:S(2)}, u32[]{:S(2)}) collective-permute-start(f32[6,128,128]{2,1,0:T(8,128)S(1)} %get-tuple-element.19), channel_id=1, source_target_pairs={{1,0},{2,1},{3,2},{4,3},{5,4},{6,5},{7,6},{0,7},{9,8},{10,9},{11,1... | collective-permute-start | bytes 1179656 | tf_op jit(solution)/shard_map/ppermute | solution.py:263
  42.1 2.0 %collective-permute-start.14 = (f32[16,24,128]{2,1,0:T(8,128)S(1)}, f32[16,24,128]{2,1,0:T(8,128)S(1)}, u32[]{:S(2)}, u32[]{:S(2)}) collective-permute-start(f32[16,24,128]{2,1,0:T(8,128)S(1)} %collective-permute-done.12.hl0), channel_id=1, source_target_pairs={{8,0},{0,8},{24,16},{16,24},{40,32},{32,40},{56,48},{48,56},{72,64... | collective-permute-start | bytes 589832 | tf_op jit(solution)/shard_map/ppermute | solution.py:237
  44.1 1.4 %collective-permute-start.15 = (f32[16,24,128]{2,1,0:T(8,128)S(1)}, f32[16,24,128]{2,1,0:T(8,128)S(1)}, u32[]{:S(2)}, u32[]{:S(2)}) collective-permute-start(f32[16,24,128]{2,1,0:T(8,128)S(1)} %collective-permute-done.13.hr0), channel_id=1, source_target_pairs={{8,0},{0,8},{24,16},{16,24},{40,32},{32,40},{56,48},{48,56},{72,64... | collective-permute-start | bytes 589832 | tf_op jit(solution)/shard_map/ppermute | solution.py:237

commit v2 on v1

v2 whole, which is shorter than its diff:
```python
import jax
import jax.numpy as jnp
import ml_dtypes
import numpy as np
from jax import lax
from jax.experimental import pallas as pl
from jax.experimental.pallas import tpu as pltpu
from jax.sharding import PartitionSpec as P

DEGREE = 3
COEFS = (
    -5369.0 / 1800.0,
    12.0 / 7.0,
    -15.0 / 56.0,
    10.0 / 189.0,
    -1.0 / 112.0,
    2.0 / 1925.0,
    -1.0 / 16632.0,
)
INVERSE_SQ = 1.0 / 0.64
UPPER_HALF = 10.0
CENTER = 10.0
FLOOR = -5.0

KIN = tuple(-0.5 * INVERSE_SQ * c for c in COEFS)
SIGMA1 = UPPER_HALF / (FLOOR - CENTER)
GAMMA = 2.0 / SIGMA1
SIGMA2 = 1.0 / (GAMMA - SIGMA1)
SIGMA3 = 1.0 / (GAMMA - SIGMA2)
STEP1 = (SIGMA1 / UPPER_HALF, None)
STEP2 = (2.0 * SIGMA2 / UPPER_HALF, SIGMA1 * SIGMA2)
STEP3 = (2.0 * SIGMA3 / UPPER_HALF, SIGMA2 * SIGMA3)

W = 6
F32 = jnp.float32
BF16 = jnp.bfloat16
SLOTS = ((0, 0), (0, 1), (3, 0), (3, 1), (-3, 0), (-3, 1))


END_SLOTS = ((0, None), (3, 0), (3, 1), (1, 0), (1, 1), (4, None), (-2, 0), (-2, 1))


def circulant(n):
    dense = np.zeros((n, n), np.float64)
    for k in range(1, W + 1):
        for i in range(n):
            dense[i, (i + k) % n] += COEFS[k] / COEFS[1]
            dense[i, (i - k) % n] += COEFS[k] / COEFS[1]
    high = dense.astype(ml_dtypes.bfloat16)
    low = (dense - high.astype(np.float64)).astype(ml_dtypes.bfloat16)
    return np.block([[high, low], [high, low]])


def in_planes(planes, left, right, out):
    n = left.shape[0] // 2
    for i in range(0, len(planes), 2):
        pair = [planes[i][...], planes[i + 1][...]]
        high = [f.astype(BF16) for f in pair]
        low = [(f - h.astype(F32)).astype(BF16) for f, h in zip(pair, high)]
        tall = jnp.concatenate([jnp.concatenate(high, 1), jnp.concatenate(low, 1)], 0)
        wide = jnp.concatenate([jnp.concatenate(high, 0), jnp.concatenate(low, 0)], 1)
        along_y = jnp.dot(left[...], tall, preferred_element_type=F32)
        along_z = jnp.dot(wide, right[...], preferred_element_type=F32)
        along_y = along_y[:n] + along_y[n:]
        along_z = along_z[:, :n] + along_z[:, n:]
        out[i] = KIN[1] * (along_y[:, :n] + along_z[:n])
        out[i + 1] = KIN[1] * (along_y[:, n:] + along_z[n:])


def over_tiles(n, body):
    def step(t, carry):
        body(pl.ds(pl.multiple_of(t * 8, 8), 8))
        return carry

    lax.fori_loop(0, n // 8, step, 0)


def along_x(vals, at, scale, total):
    for k in range(1, W + 1):
        below, above = vals.get(at - k), vals.get(at + k)
        if below is None and above is None:
            continue
        near = above if below is None else (below if above is None else below + above)
        total = total + (scale * KIN[k]) * near
    return total


def place(ref, i, steps, dh, way, out, first, planes):
    me = lax.axis_index("band")
    zz = lax.rem(me // 4 + way * steps + 8, 8)
    rows = pl.ds(pl.multiple_of(zz * 16 + (((me // 2) + dh) % 2) * 8, 8), 8)
    for p in range(planes):
        out[first + p, rows, :] = ref[i, p]


def kernel_place(mine, got, others, vown):
    way = 1 - 2 * (lax.axis_index("band") % 2)
    for ref, shift, turn in ((mine, 0, 1), (got, 1, 1), (others, -1, -1)):
        for i, (dz, dh) in enumerate(SLOTS):
            if shift + turn * dz != -4:
                place(ref, i, shift + turn * dz, dh, way, vown, 0, 16)


def kernel_own(x, left, right, w1, flat):
    in_planes([x.at[p] for p in range(16)], left, right, flat)

    def body(rows):
        vals = {p: x[p, rows, :] for p in range(16)}
        for p in range(16):
            total = flat[p, rows, :] + (3.0 * KIN[0] - CENTER) * vals[p]
            w1[p, rows, :] = along_x(vals, p, 1.0, total)

    over_tiles(x.shape[1], body)


def kernel_first(x, w1, xl, xr, vown, y1, to_left, to_right):
    alpha = STEP1[0]

    def body(rows):
        vals = {p - 12: xl[p, rows, :] for p in range(6, 12)}
        vals.update({p + 16: xr[p, rows, :] for p in range(6)})
        for p in range(16):
            total = w1[p, rows, :] + vown[p, rows, :] * x[p, rows, :]
            value = alpha * along_x(vals, p, 1.0, total)
            y1[p, rows, :] = value
            if 6 <= p < 12:
                to_left[p - 6, rows, :] = value
            if 4 <= p < 10:
                to_right[p - 4, rows, :] = value

    over_tiles(x.shape[1], body)


def kernel_before(x, xl, xr, y1, left, right, vown, side, y2, flat):
    n = x.shape[1]
    in_planes([xl.at[p + 6] for p in range(6)] + [xr.at[p] for p in range(6)], left, right, flat)

    def first_sides(rows):
        for s, start in enumerate((-6, 16)):
            vals = {
                p: xl[p + 12, rows, :] if p < 0 else (x[p, rows, :] if p < 16 else xr[p - 16, rows, :])
                for p in range(start - 6, start + 12)
            }
            for j in range(6):
                total = flat[6 * s + j, rows, :] + (3.0 * KIN[0] - CENTER) * vals[start + j]
                side[6 * s + j, rows, :] = along_x(vals, start + j, 1.0, total)

    over_tiles(n, first_sides)
    alpha, beta = STEP2
    in_planes([y1.at[p] for p in range(16)], left, right, flat)

    def second(rows):
        vals = {p: y1[p, rows, :] for p in range(16)}
        for p in range(16):
            total = flat[p, rows, :] + (vown[p, rows, :] + (3.0 * KIN[0] - CENTER)) * vals[p]
            y2[p, rows, :] = alpha * along_x(vals, p, 1.0, total) - beta * x[p, rows, :]

    over_tiles(n, second)


def kernel_middle(
    xl, xr, y1, left, right, vown, ends_l, ends_r, twin_l, twin_r, side, y2own, y2l, y2r, y3, y1s, y2, vs, flat
):
    n = y1.shape[1]
    core = lax.axis_index("band") % 2
    for refs, c in (((ends_l, ends_r), core), ((twin_l, twin_r), 1 - core)):
        for side_at, ref in enumerate(refs):
            for i, (steps, dh) in enumerate(END_SLOTS):
                place(ref, i, steps, c if dh is None else dh, 1 - 2 * c, vs, 6 * side_at, 6)

    def first(rows):
        for j in range(12):
            old = xl[6 + j, rows, :] if j < 6 else xr[j - 6, rows, :]
            y1s[j, rows, :] = STEP1[0] * (side[j, rows, :] + vs[j, rows, :] * old)

    over_tiles(n, first)
    alpha, beta = STEP2

    def second(rows):
        vals = {j - 6: y1s[j, rows, :] for j in range(6)}
        vals.update({j + 16: y1s[6 + j, rows, :] for j in range(6)})
        for p in range(16):
            y2[p, rows, :] = along_x(vals, p, alpha, y2own[p, rows, :])

    over_tiles(n, second)
    in_planes([y1s.at[p] for p in range(12)], left, right, flat)

    def second_sides(rows):
        for s, (start, low, top, dest, older) in enumerate(((-6, -6, 6, y2l, xl), (16, 10, 22, y2r, xr))):
            vals = {
                p: y1s[p + 6, rows, :] if p < 0 else (y1[p, rows, :] if p < 16 else y1s[p - 10, rows, :])
                for p in range(low, top)
            }
            for j in range(6):
                mid = vals[start + j]
                total = flat[6 * s + j, rows, :] + (vs[6 * s + j, rows, :] + (3.0 * KIN[0] - CENTER)) * mid
                old = older[j + 6 - 6 * s, rows, :]
                dest[j, rows, :] = alpha * along_x(vals, start + j, 1.0, total) - beta * old

    over_tiles(n, second_sides)
    alpha3, beta3 = STEP3
    in_planes([y2.at[p] for p in range(16)], left, right, flat)

    def third(rows):
        vals = {p: y2[p, rows, :] for p in range(16)}
        for p in range(16):
            total = flat[p, rows, :] + (vown[p, rows, :] + (3.0 * KIN[0] - CENTER)) * vals[p]
            y3[p, rows, :] = alpha3 * along_x(vals, p, 1.0, total) - beta3 * y1[p, rows, :]

    over_tiles(n, third)


def kernel_last(far_l, far_r, y2l, y2r, y3, out):
    def body(rows):
        far = {p - 12: far_l[p, rows, :] for p in range(6)}
        far.update({p + 22: far_r[p, rows, :] for p in range(6)})
        near = {}
        for j in range(6):
            near[j - 6] = along_x(far, j - 6, STEP2[0], y2l[j, rows, :])
            near[j + 16] = along_x(far, j + 16, STEP2[0], y2r[j, rows, :])
        for p in range(16):
            out[p, rows, :] = along_x(near, p, STEP3[0], y3[p, rows, :])

    over_tiles(out.shape[1], body)


def call(body, outs, scratch, args, flops):
    whole = pl.BlockSpec(memory_space=pltpu.VMEM)
    total = sum(a.size * a.dtype.itemsize for a in args) + sum(4 * int(np.prod(o)) for o in outs)
    return pl.pallas_call(
        body,
        out_shape=tuple(jax.ShapeDtypeStruct(o, F32) for o in outs),
        in_specs=[whole] * len(args),
        out_specs=tuple(whole for _ in outs),
        scratch_shapes=[pltpu.VMEM(s, F32) for s in scratch],
        compiler_params=pltpu.CompilerParams(vmem_limit_bytes=40 * 1024 * 1024),
        cost_estimate=pl.CostEstimate(flops=flops, bytes_accessed=total if flops else 0, transcendentals=0),
    )(*args)


def shards(orbital, potential):
    x = orbital[0]
    nx, ny, nz = x.shape
    bands, slabs = lax.axis_size("band"), lax.axis_size("slab")
    up = [(i, (i + 1) % slabs) for i in range(slabs)]
    down = [(b, a) for a, b in up]

    def of_band(value, source):
        return lax.ppermute(value, "band", [(source(i // 4, i // 2 % 2, i % 2), i) for i in range(bands)])

    def at(z, h, c):
        return z % (bands // 4) * 4 + h * 2 + c

    def flip(value):
        return of_band(value, lambda z, h, c: at(z, h, 1 - c))

    plane = (ny, nz)
    six, own, three = (6, *plane), (16, *plane), (3, *plane)
    cells = nx * ny * nz
    mat = circulant(ny)
    right = jnp.asarray(mat)
    left = jnp.asarray(np.ascontiguousarray(mat.T))
    core0 = lax.axis_index("band") % 2 == 0

    def in_order(mine, other, axis):
        return jnp.where(core0, jnp.concatenate([mine, other], axis), jnp.concatenate([other, mine], axis))

    block = in_order(potential, flip(potential), 1)
    last, first, held, block = lax.optimization_barrier((x[nx - 12 :], x[:12], x, block))
    part = of_band(jnp.where(core0, block[:8], block[8:]), lambda z, h, c: at(z, 1 - h, c))
    across = of_band(block, lambda z, h, c: at(z + 3 - 6 * c, 1 - h, c))
    along = of_band(block, lambda z, h, c: at(z + 3 - 6 * c, h, c))
    xl = lax.ppermute(last, "slab", up)
    xr = lax.ppermute(first, "slab", down)
    pieces = jnp.concatenate([along, across, part], 0)
    (w1,) = call(kernel_own, [own], [own], [held, left, right], 20000 * cells)
    pieces, w1 = lax.optimization_barrier((pieces, w1))
    twins = jnp.concatenate([flip(pieces[:16]), flip(pieces[16:])], 0)
    mine = jnp.stack(
        [block, in_order(part, twins[32:], 0), along, across, twins[:16], twins[16:32]], 0
    )
    gots = [of_band(mine[i : i + 2], lambda z, h, c: at(z + 1 - 2 * c, h, c)) for i in range(0, 6, 2)]
    got = jnp.concatenate(gots, 0)
    others = jnp.concatenate([flip(g) for g in gots], 0)
    xl, xr, others = lax.optimization_barrier((xl, xr, others))
    (vown,) = call(kernel_place, [own], [], [mine, got, others], 0)
    ends = jnp.stack(
        [
            jnp.where(core0, mine[0], mine[1]),
            mine[2],
            mine[3],
            got[0],
            got[1],
            jnp.where(core0, got[2], got[3]),
            got[4],
            got[5],
        ],
        0,
    )
    ends_l, ends_r = lax.ppermute(ends[:, nx - W :], "slab", up), lax.ppermute(ends[:, :W], "slab", down)

    y1, to_left, to_right = call(kernel_first, [own, six, six], [], [x, w1, xl, xr, vown], 0)
    far_r = lax.ppermute(to_left, "slab", down)
    far_l = lax.ppermute(to_right, "slab", up)
    twelve = (12, *plane)
    side, y2own = call(
        kernel_before, [twelve, own], [own], [x, xl, xr, y1, left, right, vown], 0
    )
    y2l, y2r, y3 = call(
        kernel_middle,
        [six, six, own],
        [twelve, own, twelve, own],
        [xl, xr, y1, left, right, vown, ends_l, ends_r, flip(ends_l), flip(ends_r), side, y2own],
        0,
    )
    (out,) = call(kernel_last, [own], [], [far_l, far_r, y2l, y2r, y3], 10 * cells)
    return out[None]


def solution(mesh):
    placed = (P("band", "slab", None, None), P("slab", "band", None))
    return jax.shard_map(
        shards, mesh=mesh, in_specs=placed, out_specs=P("band", "slab", None, None), check_vma=False
    )
```

time: 56 us -> 51.4 us (0.918)
  waiting for transfers between devices: 22.2 us -> 12.2 us
  starting transfers between devices: 22.1 us -> 26.5 us
    ppermute x12 -> x16, waiting for transfers between devices: 19.3 us -> 6.79 us  [the longest x14 5.57 us: of_band(): lax.ppermute(value, 'band', [(source(i // 4, i // 2 % 2, i % 2), i) for i...]
    ppermute x12 -> x16, starting transfers between devices: 15.9 us -> 22.3 us  [the longest x14 18.1 us: of_band(): lax.ppermute(value, 'band', [(source(i // 4, i // 2 % 2, i % 2), i) for i...]
    ppermute x1, starting transfers between devices: 4.19 us -> 0.08 us  [shards(): far_l = lax.ppermute(to_right, 'slab', up)]
    ppermute x1, waiting for transfers between devices: 0.01 us -> 2.22 us  [shards(): xr = lax.ppermute(first, 'slab', down)]
    ppermute x1, starting transfers between devices: 0.01 us -> 2.05 us  [shards(): far_r = lax.ppermute(to_left, 'slab', down)]
    ppermute x1, waiting for transfers between devices: 0.01 us -> 1.01 us  [shards(): far_l = lax.ppermute(to_right, 'slab', up)]
    ppermute x1, waiting for transfers between devices: 2.84 us -> 2.2 us  [shards(): far_r = lax.ppermute(to_left, 'slab', down)]
    pallas_call x4 -> x6, Pallas kernels: 9.81 us -> 10.3 us  [call(): pl.pallas_call(body, out_shape=tuple((jax.ShapeDtypeStruct(o, F32) for o...]
  transfers between devices with their start and end apart: 16 -> 20, of which waited for: 7 -> 9; matrix products, arithmetic and copies ran while one was open for 0% -> 4% of each run, Pallas kernels for 15% -> 17%
where the time goes in v2:
time: 51.4 us; the launch traced here: 51.2 us
  starting transfers between devices  26.5 us (52%)
  waiting for transfers between devices  12.2 us (24%)
  Pallas kernels  10.3 us (20%)
  local copies, waits for them, and re-layouts  1.7 us (3%)
    ppermute x14, starting transfers between devices, of_band(): lax.ppermute(value, 'band', [(source(i // 4, i // 2 % 2, i % 2), i) for i...  18.1 us
    pallas_call x6, Pallas kernels, call(): pl.pallas_call(body, out_shape=tuple((jax.ShapeDtypeStruct(o, F32) for o...  10.3 us
    ppermute x14, waiting for transfers between devices, of_band(): lax.ppermute(value, 'band', [(source(i // 4, i // 2 % 2, i % 2), i) for i...  5.57 us
    ppermute x1, starting transfers between devices, shards(): lax.ppermute(ends[:, nx - W:], 'slab', up)  3.69 us
    ppermute x1, waiting for transfers between devices, shards(): xr = lax.ppermute(first, 'slab', down)  2.22 us
    ppermute x1, waiting for transfers between devices, shards(): far_r = lax.ppermute(to_left, 'slab', down)  2.2 us
    ppermute x1, starting transfers between devices, shards(): far_r = lax.ppermute(to_left, 'slab', down)  2.05 us
    slice x1, local copies, waits for them, and re-layouts, shards(): x[:12]  1.57 us
  transfers between devices with their start and end apart: 20, of which 9 were waited for; matrix products, arithmetic and copies ran while one was open for 4% of the time, Pallas kernels for 17%

profile of v2, /device:TPU:24, one launch (start us, length us, event | category | flops | bytes accessed | tf_op | source)
XLA Modules:
  0.0 51.2 jit_solution(8863904733181574255)
XLA Ops:
  0.0 1.6 %slice_bitcast_fusion = (f32[12,128,128]{2,1,0:T(8,128)S(1)}, f32[12,128,128]{2,1,0:T(8,128)S(1)}) fusion(f32[1,16,128,128]{3,2,1,0:T(8,128)} %param.4), kind=kLoop, calls=%fused_computation | loop fusion | bytes 3145728 | tf_op jit(solution)/shard_map/slice | solution.py:269
  1.7 9.3 %collective-permute-start.2 = (f32[16,8,128]{2,1,0:T(8,128)S(1)}, f32[16,8,128]{2,1,0:T(8,128)S(1)}, u32[]{:S(2)}, u32[]{:S(2)}) collective-permute-start(f32[16,8,128]{2,1,0:T(8,128)S(1)} %maximum_select_fusion), channel_id=1, source_target_pairs={{112,0},{184,8},{96,16},{168,24},{144,32},{216,40},{128,48},{200,5... | collective-permute-start | bytes 196616 | tf_op jit(solution)/shard_map/ppermute | solution.py:249
  11.6 1.1 %collective-permute-start.4 = (f32[12,128,128]{2,1,0:T(8,128)S(1)}, f32[12,128,128]{2,1,0:T(8,128)S(1)}, u32[]{:S(2)}, u32[]{:S(2)}) collective-permute-start(f32[12,128,128]{2,1,0:T(8,128)S(1)} %get-tuple-element.25), channel_id=1, source_target_pairs={{0,1},{1,2},{2,3},{3,4},{4,5},{5,6},{6,7},{7,0},{8,9},{9,10},{10,1... | collective-permute-start | bytes 2359304 | tf_op jit(solution)/shard_map/ppermute | solution.py:273
  12.7 0.9 %collective-permute-start.5 = (f32[12,128,128]{2,1,0:T(8,128)S(1)}, f32[12,128,128]{2,1,0:T(8,128)S(1)}, u32[]{:S(2)}, u32[]{:S(2)}) collective-permute-start(f32[12,128,128]{2,1,0:T(8,128)S(1)} %get-tuple-element.26), channel_id=1, source_target_pairs={{1,0},{2,1},{3,2},{4,3},{5,4},{6,5},{7,6},{0,7},{9,8},{10,9},{11,1... | collective-permute-start | bytes 2359304 | tf_op jit(solution)/shard_map/ppermute | solution.py:274
  13.7 1.4 %shard_map.46.w1 = f32[16,128,128]{2,1,0:T(8,128)S(1)} custom-call(f32[16,128,128]{2,1,0:T(8,128)S(1)} %bitcast.27, bf16[256,256]{1,0:T(8,128)(2,1)S(1)} %copy-done.1, bf16[256,256]{1,0:T(8,128)(2,1)S(1)} %copy-done.2), custom_call_target="tpu_custom_call" | custom-call | flops 5242880000 | bytes 2359296 | tf_op jit(solution)/shard_map/pallas_call | solution.py:230
  15.1 1.4 %collective-permute-done.3 = f32[8,8,128]{2,1,0:T(8,128)S(1)} collective-permute-done((f32[8,8,128]{2,1,0:T(8,128)S(1)}, f32[8,8,128]{2,1,0:T(8,128)S(1)}, u32[]{:S(2)}, u32[]{:S(2)}) %collective-permute-start.3) | collective-permute-done | bytes 32800 | tf_op jit(solution)/shard_map/ppermute | solution.py:249
  16.5 0.6 %collective-permute-done.1 = f32[16,8,128]{2,1,0:T(8,128)S(1)} collective-permute-done((f32[16,8,128]{2,1,0:T(8,128)S(1)}, f32[16,8,128]{2,1,0:T(8,128)S(1)}, u32[]{:S(2)}, u32[]{:S(2)}) %collective-permute-start.1) | collective-permute-done | bytes 65568 | tf_op jit(solution)/shard_map/ppermute | solution.py:249
  17.4 2.8 %collective-permute-start.9 = (f32[2,16,8,128]{3,2,1,0:T(8,128)S(1)}, f32[2,16,8,128]{3,2,1,0:T(8,128)S(1)}, u32[]{:S(2)}, u32[]{:S(2)}) collective-permute-start(f32[2,16,8,128]{3,2,1,0:T(8,128)S(1)} %pad_maximum_fusion.4), channel_id=1, source_target_pairs={{32,0},{232,8},{48,16},{248,24},{64,32},{8,40},{80,48},{24,56},{96... | collective-permute-start | bytes 393224 | tf_op jit(solution)/shard_map/ppermute | solution.py:249
  20.4 1.0 %collective-permute-done.11 = f32[16,8,128]{2,1,0:T(8,128)S(1)} collective-permute-done((f32[16,8,128]{2,1,0:T(8,128)S(1)}, f32[16,8,128]{2,1,0:T(8,128)S(1)}, u32[]{:S(2)}, u32[]{:S(2)}) %collective-permute-start.11) | collective-permute-done | bytes 65568 | tf_op jit(solution)/shard_map/ppermute | solution.py:249
  21.5 1.2 %collective-permute-start.12 = (f32[2,16,8,128]{3,2,1,0:T(8,128)S(1)}, f32[2,16,8,128]{3,2,1,0:T(8,128)S(1)}, u32[]{:S(2)}, u32[]{:S(2)}) collective-permute-start(f32[2,16,8,128]{3,2,1,0:T(8,128)S(1)} %pad_maximum_fusion.5), channel_id=1, source_target_pairs={{32,0},{232,8},{48,16},{248,24},{64,32},{8,40},{80,48},{24,56},{96... | collective-permute-start | bytes 393224 | tf_op jit(solution)/shard_map/ppermute | solution.py:249
  22.8 1.9 %collective-permute-start.7 = (f32[2,16,8,128]{3,2,1,0:T(8,128)S(1)}, f32[2,16,8,128]{3,2,1,0:T(8,128)S(1)}, u32[]{:S(2)}, u32[]{:S(2)}) collective-permute-start(f32[2,16,8,128]{3,2,1,0:T(8,128)S(1)} %pad_maximum_fusion.3), channel_id=1, source_target_pairs={{32,0},{232,8},{48,16},{248,24},{64,32},{8,40},{80,48},{24,56},{96... | collective-permute-start | bytes 393224 | tf_op jit(solution)/shard_map/ppermute | solution.py:249
  24.9 1.6 %collective-permute-done.12 = f32[2,16,8,128]{3,2,1,0:T(8,128)S(1)} collective-permute-done((f32[2,16,8,128]{3,2,1,0:T(8,128)S(1)}, f32[2,16,8,128]{3,2,1,0:T(8,128)S(1)}, u32[]{:S(2)}, u32[]{:S(2)}) %collective-permute-start.12) | collective-permute-done | bytes 131104 | tf_op jit(solution)/shard_map/ppermute | solution.py:249
  26.5 0.6 %collective-permute-start.13 = (f32[2,16,8,128]{3,2,1,0:T(8,128)S(1)}, f32[2,16,8,128]{3,2,1,0:T(8,128)S(1)}, u32[]{:S(2)}, u32[]{:S(2)}) collective-permute-start(f32[2,16,8,128]{3,2,1,0:T(8,128)S(1)} %collective-permute-done.12), channel_id=1, source_target_pairs={{8,0},{0,8},{24,16},{16,24},{40,32},{32,40},{56,48},{48,56},{72,64... | collective-permute-start | bytes 393224 | tf_op jit(solution)/shard_map/ppermute | solution.py:249
  27.1 0.8 %collective-permute-done.7 = f32[2,16,8,128]{3,2,1,0:T(8,128)S(1)} collective-permute-done((f32[2,16,8,128]{3,2,1,0:T(8,128)S(1)}, f32[2,16,8,128]{3,2,1,0:T(8,128)S(1)}, u32[]{:S(2)}, u32[]{:S(2)}) %collective-permute-start.7) | collective-permute-done | bytes 131104 | tf_op jit(solution)/shard_map/ppermute | solution.py:249
  29.2 3.7 %collective-permute-start.16 = (f32[8,6,8,128]{3,2,1,0:T(8,128)S(1)}, f32[8,6,8,128]{3,2,1,0:T(8,128)S(1)}, u32[]{:S(2)}, u32[]{:S(2)}) collective-permute-start(f32[8,6,8,128]{3,2,1,0:T(8,128)S(1)} %get-tuple-element.44), channel_id=1, source_target_pairs={{0,1},{1,2},{2,3},{3,4},{4,5},{5,6},{6,7},{7,0},{8,9},{9,10},{10,1... | collective-permute-start | bytes 589832 | tf_op jit(solution)/shard_map/ppermute | solution.py:300
  32.9 2.2 %collective-permute-done.5.xr = f32[12,128,128]{2,1,0:T(8,128)S(1)} collective-permute-done((f32[12,128,128]{2,1,0:T(8,128)S(1)}, f32[12,128,128]{2,1,0:T(8,128)S(1)}, u32[]{:S(2)}, u32[]{:S(2)}) %collective-permute-start.5) | collective-permute-done | bytes 786464 | tf_op jit(solution)/shard_map/ppermute | solution.py:274
  35.2 0.7 %shard_map.48 = (f32[16,128,128]{2,1,0:T(8,128)S(1)}, f32[6,128,128]{2,1,0:T(8,128)S(1)}, f32[6,128,128]{2,1,0:T(8,128)S(1)}) custom-call(f32[16,128,128]{2,1,0:T(8,128)S(1)} %bitcast.28, f32[16,128,128]{2,1,0:T(8,128)S(1)} %shard_map.46.w1, f32[12,128,128]{2,1,0:T(8,128)S(1)} %collective-permute-done.4.xl, f32[12,128,128]{2,1,0:T(8,128)S(1)} %collective-permute-done.5.xr, ...), custom_call_target="tpu_custom_call" | custom-call | tf_op jit(solution)/shard_map/pallas_call | solution.py:230
  36.1 2.0 %collective-permute-start.15 = (f32[6,128,128]{2,1,0:T(8,128)S(1)}, f32[6,128,128]{2,1,0:T(8,128)S(1)}, u32[]{:S(2)}, u32[]{:S(2)}) collective-permute-start(f32[6,128,128]{2,1,0:T(8,128)S(1)} %get-tuple-element.32), channel_id=1, source_target_pairs={{1,0},{2,1},{3,2},{4,3},{5,4},{6,5},{7,6},{0,7},{9,8},{10,9},{11,1... | collective-permute-start | bytes 1179656 | tf_op jit(solution)/shard_map/ppermute | solution.py:303
  38.1 1.2 %collective-permute-done.17.ends_r = f32[8,6,8,128]{3,2,1,0:T(8,128)S(1)} collective-permute-done((f32[8,6,8,128]{3,2,1,0:T(8,128)S(1)}, f32[8,6,8,128]{3,2,1,0:T(8,128)S(1)}, u32[]{:S(2)}, u32[]{:S(2)}) %collective-permute-start.17) | collective-permute-done | bytes 196640 | tf_op jit(solution)/shard_map/ppermute | solution.py:300
  39.8 2.8 %shard_map.49 = (f32[12,128,128]{2,1,0:T(8,128)S(1)}, f32[16,128,128]{2,1,0:T(8,128)S(1)}) custom-call(f32[16,128,128]{2,1,0:T(8,128)S(1)} %bitcast.29, f32[12,128,128]{2,1,0:T(8,128)S(1)} %collective-permute-done.4.xl, f32[12,128,128]{2,1,0:T(8,128)S(1)} %collective-permute-done.5.xr, f32[16,128,128]{2,1,0:T(8,128)S(1)} %get-tuple-element.33.y1, ...), custom_call_target="tpu_custom_call" | custom-call | tf_op jit(solution)/shard_map/pallas_call | solution.py:230
  42.7 3.8 %shard_map.50 = (f32[6,128,128]{2,1,0:T(8,128)S(1)}, f32[6,128,128]{2,1,0:T(8,128)S(1)}, f32[16,128,128]{2,1,0:T(8,128)S(1)}) custom-call(f32[12,128,128]{2,1,0:T(8,128)S(1)} %collective-permute-done.4.xl, f32[12,128,128]{2,1,0:T(8,128)S(1)} %collective-permute-done.5.xr, f32[16,128,128]{2,1,0:T(8,128)S(1)} %get-tuple-element.33.y1, ...), custom_call_target="tpu_custom_call" | custom-call | tf_op jit(solution)/shard_map/pallas_call | solution.py:230
  46.5 1.0 %collective-permute-done.14.far_l = f32[6,128,128]{2,1,0:T(8,128)S(1)} collective-permute-done((f32[6,128,128]{2,1,0:T(8,128)S(1)}, f32[6,128,128]{2,1,0:T(8,128)S(1)}, u32[]{:S(2)}, u32[]{:S(2)}) %collective-permute-start.14) | collective-permute-done | bytes 393248 | tf_op jit(solution)/shard_map/ppermute | solution.py:304
  47.5 2.2 %collective-permute-done.15.far_r = f32[6,128,128]{2,1,0:T(8,128)S(1)} collective-permute-done((f32[6,128,128]{2,1,0:T(8,128)S(1)}, f32[6,128,128]{2,1,0:T(8,128)S(1)}, u32[]{:S(2)}, u32[]{:S(2)}) %collective-permute-start.15) | collective-permute-done | bytes 393248 | tf_op jit(solution)/shard_map/ppermute | solution.py:303
  49.7 1.5 %shard_map.51 = f32[16,128,128]{2,1,0:T(8,128)} custom-call(f32[6,128,128]{2,1,0:T(8,128)S(1)} %collective-permute-done.14.far_l, f32[6,128,128]{2,1,0:T(8,128)S(1)} %collective-permute-done.15.far_r, f32[6,128,128]{2,1,0:T(8,128)S(1)} %get-tuple-element.36.y2l, f32[6,128,128]{2,1,0:T(8,128)S(1)} %get-tuple-element.37.y2r, ...), custom_call_target="tpu_custom_call" | custom-call | flops 2621440 | bytes 3670016 | tf_op jit(solution)/shard_map/pallas_call | solution.py:230
  (53 shorter events, 3.3 us)
Async XLA Ops:
  0.0 13.7 %copy-start = (f32[1,16,128,128]{3,2,1,0:T(8,128)S(1)}, f32[1,16,128,128]{3,2,1,0:T(8,128)}, u32[]{:S(2)}) copy-start(f32[1,16,128,128]{3,2,1,0:T(8,128)} %param.4) | copy-start | bytes 3145732
  0.0 1.6 %collective-permute-start = (f32[16,4,128]{2,1,0:T(4,128)}, f32[16,4,128]{2,1,0:T(4,128)S(1)}, u32[]{:S(2)}, u32[]{:S(2)}) collective-permute-start(f32[16,4,128]{2,1,0:T(4,128)} %param.5), channel_id=1, source_target_pairs={{8,0},{0,8},{24,16},{16,24},{40,32},{32,40},{56,48},{48,56},{72,64... | collective-permute-start | bytes 98312 | tf_op jit(solution)/shard_map/ppermute | solution.py:249
  0.0 1.6 %copy-start.3 = (f32[16,4,128]{2,1,0:T(4,128)S(1)}, f32[16,4,128]{2,1,0:T(4,128)}, u32[]{:S(2)}) copy-start(f32[16,4,128]{2,1,0:T(4,128)} %param.5) | copy-start | bytes 98308
  1.6 12.1 %copy-start.2 = (bf16[256,256]{1,0:T(8,128)(2,1)S(1)}, bf16[256,256]{1,0:T(8,128)(2,1)}, u32[]{:S(2)}) copy-start(bf16[256,256]{1,0:T(8,128)(2,1)} %constant.24.clone.right) | copy-start | bytes 393220
  1.6 12.1 %copy-start.1 = (bf16[256,256]{1,0:T(8,128)(2,1)S(1)}, bf16[256,256]{1,0:T(8,128)(2,1)}, u32[]{:S(2)}) copy-start(bf16[256,256]{1,0:T(8,128)(2,1)} %constant.25.clone.left) | copy-start | bytes 393220
  1.7 14.8 %collective-permute-start.2 = (f32[16,8,128]{2,1,0:T(8,128)S(1)}, f32[16,8,128]{2,1,0:T(8,128)S(1)}, u32[]{:S(2)}, u32[]{:S(2)}) collective-permute-start(f32[16,8,128]{2,1,0:T(8,128)S(1)} %maximum_select_fusion), channel_id=1, source_target_pairs={{112,0},{184,8},{96,16},{168,24},{144,32},{216,40},{128,48},{200,5... | collective-permute-start | bytes 196616 | tf_op jit(solution)/shard_map/ppermute | solution.py:249
  11.0 6.2 %collective-permute-start.1 = (f32[16,8,128]{2,1,0:T(8,128)S(1)}, f32[16,8,128]{2,1,0:T(8,128)S(1)}, u32[]{:S(2)}, u32[]{:S(2)}) collective-permute-start(f32[16,8,128]{2,1,0:T(8,128)S(1)} %maximum_select_fusion), channel_id=1, source_target_pairs={{96,0},{168,8},{112,16},{184,24},{128,32},{200,40},{144,48},{216,5... | collective-permute-start | bytes 196616 | tf_op jit(solution)/shard_map/ppermute | solution.py:249
  11.1 5.4 %collective-permute-start.3 = (f32[8,8,128]{2,1,0:T(8,128)S(1)}, f32[8,8,128]{2,1,0:T(8,128)S(1)}, u32[]{:S(2)}, u32[]{:S(2)}) collective-permute-start(f32[8,8,128]{2,1,0:T(8,128)S(1)} %slice_select_fusion.1), channel_id=1, source_target_pairs={{16,0},{24,8},{0,16},{8,24},{48,32},{56,40},{32,48},{40,56},{80,64... | collective-permute-start | bytes 98312 | tf_op jit(solution)/shard_map/ppermute | solution.py:249
  11.6 21.3 %collective-permute-start.4 = (f32[12,128,128]{2,1,0:T(8,128)S(1)}, f32[12,128,128]{2,1,0:T(8,128)S(1)}, u32[]{:S(2)}, u32[]{:S(2)}) collective-permute-start(f32[12,128,128]{2,1,0:T(8,128)S(1)} %get-tuple-element.25), channel_id=1, source_target_pairs={{0,1},{1,2},{2,3},{3,4},{4,5},{5,6},{6,7},{7,0},{8,9},{9,10},{10,1... | collective-permute-start | bytes 2359304 | tf_op jit(solution)/shard_map/ppermute | solution.py:273
  12.7 22.4 %collective-permute-start.5 = (f32[12,128,128]{2,1,0:T(8,128)S(1)}, f32[12,128,128]{2,1,0:T(8,128)S(1)}, u32[]{:S(2)}, u32[]{:S(2)}) collective-permute-start(f32[12,128,128]{2,1,0:T(8,128)S(1)} %get-tuple-element.26), channel_id=1, source_target_pairs={{1,0},{2,1},{3,2},{4,3},{5,4},{6,5},{7,6},{0,7},{9,8},{10,9},{11,1... | collective-permute-start | bytes 2359304 | tf_op jit(solution)/shard_map/ppermute | solution.py:274
  17.2 3.2 %collective-permute-start.6 = (f32[24,8,128]{2,1,0:T(8,128)S(1)}, f32[24,8,128]{2,1,0:T(8,128)S(1)}, u32[]{:S(2)}, u32[]{:S(2)}) collective-permute-start(f32[24,8,128]{2,1,0:T(8,128)S(1)} %slice.60), channel_id=1, source_target_pairs={{8,0},{0,8},{24,16},{16,24},{40,32},{32,40},{56,48},{48,56},{72,64... | collective-permute-start | bytes 294920 | tf_op jit(solution)/shard_map/ppermute | solution.py:249
  17.4 7.4 %collective-permute-start.9 = (f32[2,16,8,128]{3,2,1,0:T(8,128)S(1)}, f32[2,16,8,128]{3,2,1,0:T(8,128)S(1)}, u32[]{:S(2)}, u32[]{:S(2)}) collective-permute-start(f32[2,16,8,128]{3,2,1,0:T(8,128)S(1)} %pad_maximum_fusion.4), channel_id=1, source_target_pairs={{32,0},{232,8},{48,16},{248,24},{64,32},{8,40},{80,48},{24,56},{96... | collective-permute-start | bytes 393224 | tf_op jit(solution)/shard_map/ppermute | solution.py:249
  20.2 1.3 %collective-permute-start.11 = (f32[16,8,128]{2,1,0:T(8,128)S(1)}, f32[16,8,128]{2,1,0:T(8,128)S(1)}, u32[]{:S(2)}, u32[]{:S(2)}) collective-permute-start(f32[16,8,128]{2,1,0:T(8,128)S(1)} %slice.62), channel_id=1, source_target_pairs={{8,0},{0,8},{24,16},{16,24},{40,32},{32,40},{56,48},{48,56},{72,64... | collective-permute-start | bytes 196616 | tf_op jit(solution)/shard_map/ppermute | solution.py:249
  21.5 5.0 %collective-permute-start.12 = (f32[2,16,8,128]{3,2,1,0:T(8,128)S(1)}, f32[2,16,8,128]{3,2,1,0:T(8,128)S(1)}, u32[]{:S(2)}, u32[]{:S(2)}) collective-permute-start(f32[2,16,8,128]{3,2,1,0:T(8,128)S(1)} %pad_maximum_fusion.5), channel_id=1, source_target_pairs={{32,0},{232,8},{48,16},{248,24},{64,32},{8,40},{80,48},{24,56},{96... | collective-permute-start | bytes 393224 | tf_op jit(solution)/shard_map/ppermute | solution.py:249
  22.8 5.2 %collective-permute-start.7 = (f32[2,16,8,128]{3,2,1,0:T(8,128)S(1)}, f32[2,16,8,128]{3,2,1,0:T(8,128)S(1)}, u32[]{:S(2)}, u32[]{:S(2)}) collective-permute-start(f32[2,16,8,128]{3,2,1,0:T(8,128)S(1)} %pad_maximum_fusion.3), channel_id=1, source_target_pairs={{32,0},{232,8},{48,16},{248,24},{64,32},{8,40},{80,48},{24,56},{96... | collective-permute-start | bytes 393224 | tf_op jit(solution)/shard_map/ppermute | solution.py:249
  24.8 3.8 %collective-permute-start.10 = (f32[2,16,8,128]{3,2,1,0:T(8,128)S(1)}, f32[2,16,8,128]{3,2,1,0:T(8,128)S(1)}, u32[]{:S(2)}, u32[]{:S(2)}) collective-permute-start(f32[2,16,8,128]{3,2,1,0:T(8,128)S(1)} %collective-permute-done.9), channel_id=1, source_target_pairs={{8,0},{0,8},{24,16},{16,24},{40,32},{32,40},{56,48},{48,56},{72,64... | collective-permute-start | bytes 393224 | tf_op jit(solution)/shard_map/ppermute | solution.py:249
  26.5 2.6 %collective-permute-start.13 = (f32[2,16,8,128]{3,2,1,0:T(8,128)S(1)}, f32[2,16,8,128]{3,2,1,0:T(8,128)S(1)}, u32[]{:S(2)}, u32[]{:S(2)}) collective-permute-start(f32[2,16,8,128]{3,2,1,0:T(8,128)S(1)} %collective-permute-done.12), channel_id=1, source_target_pairs={{8,0},{0,8},{24,16},{16,24},{40,32},{32,40},{56,48},{48,56},{72,64... | collective-permute-start | bytes 393224 | tf_op jit(solution)/shard_map/ppermute | solution.py:249
  27.9 4.9 %collective-permute-start.8 = (f32[2,16,8,128]{3,2,1,0:T(8,128)S(1)}, f32[2,16,8,128]{3,2,1,0:T(8,128)S(1)}, u32[]{:S(2)}, u32[]{:S(2)}) collective-permute-start(f32[2,16,8,128]{3,2,1,0:T(8,128)S(1)} %collective-permute-done.7), channel_id=1, source_target_pairs={{8,0},{0,8},{24,16},{16,24},{40,32},{32,40},{56,48},{48,56},{72,64... | collective-permute-start | bytes 393224 | tf_op jit(solution)/shard_map/ppermute | solution.py:249
  28.6 10.7 %collective-permute-start.17 = (f32[8,6,8,128]{3,2,1,0:T(8,128)S(1)}, f32[8,6,8,128]{3,2,1,0:T(8,128)S(1)}, u32[]{:S(2)}, u32[]{:S(2)}) collective-permute-start(f32[8,6,8,128]{3,2,1,0:T(8,128)S(1)} %get-tuple-element.43), channel_id=1, source_target_pairs={{1,0},{2,1},{3,2},{4,3},{5,4},{6,5},{7,6},{0,7},{9,8},{10,9},{11,1... | collective-permute-start | bytes 589832 | tf_op jit(solution)/shard_map/ppermute | solution.py:300
  29.2 10.3 %collective-permute-start.16 = (f32[8,6,8,128]{3,2,1,0:T(8,128)S(1)}, f32[8,6,8,128]{3,2,1,0:T(8,128)S(1)}, u32[]{:S(2)}, u32[]{:S(2)}) collective-permute-start(f32[8,6,8,128]{3,2,1,0:T(8,128)S(1)} %get-tuple-element.44), channel_id=1, source_target_pairs={{0,1},{1,2},{2,3},{3,4},{4,5},{5,6},{6,7},{7,0},{8,9},{9,10},{10,1... | collective-permute-start | bytes 589832 | tf_op jit(solution)/shard_map/ppermute | solution.py:300
  36.0 11.5 %collective-permute-start.14 = (f32[6,128,128]{2,1,0:T(8,128)S(1)}, f32[6,128,128]{2,1,0:T(8,128)S(1)}, u32[]{:S(2)}, u32[]{:S(2)}) collective-permute-start(f32[6,128,128]{2,1,0:T(8,128)S(1)} %get-tuple-element.31), channel_id=1, source_target_pairs={{0,1},{1,2},{2,3},{3,4},{4,5},{5,6},{6,7},{7,0},{8,9},{9,10},{10,1... | collective-permute-start | bytes 1179656 | tf_op jit(solution)/shard_map/ppermute | solution.py:304
  36.1 13.6 %collective-permute-start.15 = (f32[6,128,128]{2,1,0:T(8,128)S(1)}, f32[6,128,128]{2,1,0:T(8,128)S(1)}, u32[]{:S(2)}, u32[]{:S(2)}) collective-permute-start(f32[6,128,128]{2,1,0:T(8,128)S(1)} %get-tuple-element.32), channel_id=1, source_target_pairs={{1,0},{2,1},{3,2},{4,3},{5,4},{6,5},{7,6},{0,7},{9,8},{10,9},{11,1... | collective-permute-start | bytes 1179656 | tf_op jit(solution)/shard_map/ppermute | solution.py:303
  39.3 3.3 %collective-permute-start.19 = (f32[8,6,8,128]{3,2,1,0:T(8,128)S(1)}, f32[8,6,8,128]{3,2,1,0:T(8,128)S(1)}, u32[]{:S(2)}, u32[]{:S(2)}) collective-permute-start(f32[8,6,8,128]{3,2,1,0:T(8,128)S(1)} %collective-permute-done.17.ends_r), channel_id=1, source_target_pairs={{8,0},{0,8},{24,16},{16,24},{40,32},{32,40},{56,48},{48,56},{72,64... | collective-permute-start | bytes 589832 | tf_op jit(solution)/shard_map/ppermute | solution.py:249
  39.5 3.2 %collective-permute-start.18 = (f32[8,6,8,128]{3,2,1,0:T(8,128)S(1)}, f32[8,6,8,128]{3,2,1,0:T(8,128)S(1)}, u32[]{:S(2)}, u32[]{:S(2)}) collective-permute-start(f32[8,6,8,128]{3,2,1,0:T(8,128)S(1)} %collective-permute-done.16.ends_l), channel_id=1, source_target_pairs={{8,0},{0,8},{24,16},{16,24},{40,32},{32,40},{56,48},{48,56},{72,64... | collective-permute-start | bytes 589832 | tf_op jit(solution)/shard_map/ppermute | solution.py:249

commit v3 on v2

--- a/solution.py
+++ b/solution.py
@@ -210,18 +210,28 @@
     over_tiles(n, third)
 
 
-def kernel_last(far_l, far_r, y2l, y2r, y3, out):
-    def body(rows):
-        far = {p - 12: far_l[p, rows, :] for p in range(6)}
-        far.update({p + 22: far_r[p, rows, :] for p in range(6)})
-        near = {}
-        for j in range(6):
-            near[j - 6] = along_x(far, j - 6, STEP2[0], y2l[j, rows, :])
-            near[j + 16] = along_x(far, j + 16, STEP2[0], y2r[j, rows, :])
-        for p in range(16):
-            out[p, rows, :] = along_x(near, p, STEP3[0], y3[p, rows, :])
-
-    over_tiles(out.shape[1], body)
+def kernel_last(far_l, far_r, y2l, y2r, y3, out, done, sems):
+    def leave(source, start, stop, at):
+        copy = pltpu.make_async_copy(source.at[start:stop], out.at[start:stop], sems.at[at])
+        copy.start()
+        return copy
+
+    def side(far_ref, far_start, y2_ref, y2_start, first, last):
+        def body(rows):
+            far = {far_start + j: far_ref[j, rows, :] for j in range(W)}
+            near = {y2_start + j: along_x(far, y2_start + j, STEP2[0], y2_ref[j, rows, :]) for j in range(W)}
+            for p in range(first, last):
+                done[p, rows, :] = along_x(near, p, STEP3[0], y3[p, rows, :])
+
+        over_tiles(done.shape[1], body)
+
+    copies = [leave(y3, W, 16 - W, 0)]
+    side(far_l, -12, y2l, -6, 0, W)
+    copies.append(leave(done, 0, W, 1))
+    side(far_r, 22, y2r, 16, 16 - W, 16)
+    copies.append(leave(done, 16 - W, 16, 2))
+    for copy in copies:
+        copy.wait()
 
 
 def call(body, outs, scratch, args, flops):
@@ -313,7 +323,15 @@
         [xl, xr, y1, left, right, vown, ends_l, ends_r, flip(ends_l), flip(ends_r), side, y2own],
         0,
     )
-    (out,) = call(kernel_last, [own], [], [far_l, far_r, y2l, y2r, y3], 10 * cells)
+    out = pl.pallas_call(
+        kernel_last,
+        out_shape=jax.ShapeDtypeStruct(own, F32),
+        in_specs=[pl.BlockSpec(memory_space=pltpu.VMEM)] * 5,
+        out_specs=pl.BlockSpec(memory_space=pl.ANY),
+        scratch_shapes=[pltpu.VMEM(own, F32), pltpu.SemaphoreType.DMA((3,))],
+        compiler_params=pltpu.CompilerParams(vmem_limit_bytes=40 * 1024 * 1024),
+        cost_estimate=pl.CostEstimate(flops=10 * cells, bytes_accessed=8 * cells, transcendentals=0),
+    )(far_l, far_r, y2l, y2r, y3)
     return out[None]
 
 

time: 51.4 us -> 51.4 us (level)
    pallas_call x6 -> x5, Pallas kernels: 10.3 us -> 8.82 us  [call(): pl.pallas_call(body, out_shape=tuple((jax.ShapeDtypeStruct(o, F32) for o...]
    pallas_call x0 -> x1, Pallas kernels: none -> 1.36 us  [shards(): pl.pallas_call(kernel_last, out_shape=jax.ShapeDtypeStruct(own, F32), in_...]
where the time goes in v3:
time: 51.4 us; the launch traced here: 51.2 us
  starting transfers between devices  26.5 us (52%)
  waiting for transfers between devices  12.2 us (24%)
  Pallas kernels  10.2 us (20%)
  local copies, waits for them, and re-layouts  1.7 us (3%)
    ppermute x14, starting transfers between devices, of_band(): lax.ppermute(value, 'band', [(source(i // 4, i // 2 % 2, i % 2), i) for i...  18.1 us
    pallas_call x5, Pallas kernels, call(): pl.pallas_call(body, out_shape=tuple((jax.ShapeDtypeStruct(o, F32) for o...  8.82 us
    ppermute x14, waiting for transfers between devices, of_band(): lax.ppermute(value, 'band', [(source(i // 4, i // 2 % 2, i % 2), i) for i...  5.57 us
    ppermute x1, starting transfers between devices, shards(): lax.ppermute(ends[:, nx - W:], 'slab', up)  3.69 us
    ppermute x1, waiting for transfers between devices, shards(): xr = lax.ppermute(first, 'slab', down)  2.22 us
    ppermute x1, waiting for transfers between devices, shards(): far_r = lax.ppermute(to_left, 'slab', down)  2.2 us
    ppermute x1, starting transfers between devices, shards(): far_r = lax.ppermute(to_left, 'slab', down)  2.05 us
    slice x1, local copies, waits for them, and re-layouts, shards(): x[:12]  1.57 us
  transfers between devices with their start and end apart: 20, of which 9 were waited for; matrix products, arithmetic and copies ran while one was open for 4% of the time, Pallas kernels for 17%

profile of v3, /device:TPU:24, one launch (start us, length us, event | category | flops | bytes accessed | tf_op | source)
XLA Modules:
  0.0 51.2 jit_solution(867774464116669635)
XLA Ops:
  0.0 1.6 %slice_bitcast_fusion = (f32[12,128,128]{2,1,0:T(8,128)S(1)}, f32[12,128,128]{2,1,0:T(8,128)S(1)}) fusion(f32[1,16,128,128]{3,2,1,0:T(8,128)} %param.4), kind=kLoop, calls=%fused_computation | loop fusion | bytes 3145728 | tf_op jit(solution)/shard_map/slice | solution.py:279
  1.7 9.3 %collective-permute-start.2 = (f32[16,8,128]{2,1,0:T(8,128)S(1)}, f32[16,8,128]{2,1,0:T(8,128)S(1)}, u32[]{:S(2)}, u32[]{:S(2)}) collective-permute-start(f32[16,8,128]{2,1,0:T(8,128)S(1)} %maximum_select_fusion), channel_id=1, source_target_pairs={{112,0},{184,8},{96,16},{168,24},{144,32},{216,40},{128,48},{200,5... | collective-permute-start | bytes 196616 | tf_op jit(solution)/shard_map/ppermute | solution.py:259
  11.6 1.1 %collective-permute-start.4 = (f32[12,128,128]{2,1,0:T(8,128)S(1)}, f32[12,128,128]{2,1,0:T(8,128)S(1)}, u32[]{:S(2)}, u32[]{:S(2)}) collective-permute-start(f32[12,128,128]{2,1,0:T(8,128)S(1)} %get-tuple-element.25), channel_id=1, source_target_pairs={{0,1},{1,2},{2,3},{3,4},{4,5},{5,6},{6,7},{7,0},{8,9},{9,10},{10,1... | collective-permute-start | bytes 2359304 | tf_op jit(solution)/shard_map/ppermute | solution.py:283
  12.7 0.9 %collective-permute-start.5 = (f32[12,128,128]{2,1,0:T(8,128)S(1)}, f32[12,128,128]{2,1,0:T(8,128)S(1)}, u32[]{:S(2)}, u32[]{:S(2)}) collective-permute-start(f32[12,128,128]{2,1,0:T(8,128)S(1)} %get-tuple-element.26), channel_id=1, source_target_pairs={{1,0},{2,1},{3,2},{4,3},{5,4},{6,5},{7,6},{0,7},{9,8},{10,9},{11,1... | collective-permute-start | bytes 2359304 | tf_op jit(solution)/shard_map/ppermute | solution.py:284
  13.7 1.4 %shard_map.46.w1 = f32[16,128,128]{2,1,0:T(8,128)S(1)} custom-call(f32[16,128,128]{2,1,0:T(8,128)S(1)} %bitcast.27, bf16[256,256]{1,0:T(8,128)(2,1)S(1)} %copy-done.1, bf16[256,256]{1,0:T(8,128)(2,1)S(1)} %copy-done.2), custom_call_target="tpu_custom_call" | custom-call | flops 5242880000 | bytes 2359296 | tf_op jit(solution)/shard_map/pallas_call | solution.py:240
  15.1 1.4 %collective-permute-done.3 = f32[8,8,128]{2,1,0:T(8,128)S(1)} collective-permute-done((f32[8,8,128]{2,1,0:T(8,128)S(1)}, f32[8,8,128]{2,1,0:T(8,128)S(1)}, u32[]{:S(2)}, u32[]{:S(2)}) %collective-permute-start.3) | collective-permute-done | bytes 32800 | tf_op jit(solution)/shard_map/ppermute | solution.py:259
  16.5 0.6 %collective-permute-done.1 = f32[16,8,128]{2,1,0:T(8,128)S(1)} collective-permute-done((f32[16,8,128]{2,1,0:T(8,128)S(1)}, f32[16,8,128]{2,1,0:T(8,128)S(1)}, u32[]{:S(2)}, u32[]{:S(2)}) %collective-permute-start.1) | collective-permute-done | bytes 65568 | tf_op jit(solution)/shard_map/ppermute | solution.py:259
  17.4 2.8 %collective-permute-start.9 = (f32[2,16,8,128]{3,2,1,0:T(8,128)S(1)}, f32[2,16,8,128]{3,2,1,0:T(8,128)S(1)}, u32[]{:S(2)}, u32[]{:S(2)}) collective-permute-start(f32[2,16,8,128]{3,2,1,0:T(8,128)S(1)} %pad_maximum_fusion.4), channel_id=1, source_target_pairs={{32,0},{232,8},{48,16},{248,24},{64,32},{8,40},{80,48},{24,56},{96... | collective-permute-start | bytes 393224 | tf_op jit(solution)/shard_map/ppermute | solution.py:259
  20.4 1.0 %collective-permute-done.11 = f32[16,8,128]{2,1,0:T(8,128)S(1)} collective-permute-done((f32[16,8,128]{2,1,0:T(8,128)S(1)}, f32[16,8,128]{2,1,0:T(8,128)S(1)}, u32[]{:S(2)}, u32[]{:S(2)}) %collective-permute-start.11) | collective-permute-done | bytes 65568 | tf_op jit(solution)/shard_map/ppermute | solution.py:259
  21.5 1.2 %collective-permute-start.12 = (f32[2,16,8,128]{3,2,1,0:T(8,128)S(1)}, f32[2,16,8,128]{3,2,1,0:T(8,128)S(1)}, u32[]{:S(2)}, u32[]{:S(2)}) collective-permute-start(f32[2,16,8,128]{3,2,1,0:T(8,128)S(1)} %pad_maximum_fusion.5), channel_id=1, source_target_pairs={{32,0},{232,8},{48,16},{248,24},{64,32},{8,40},{80,48},{24,56},{96... | collective-permute-start | bytes 393224 | tf_op jit(solution)/shard_map/ppermute | solution.py:259
  22.8 1.9 %collective-permute-start.7 = (f32[2,16,8,128]{3,2,1,0:T(8,128)S(1)}, f32[2,16,8,128]{3,2,1,0:T(8,128)S(1)}, u32[]{:S(2)}, u32[]{:S(2)}) collective-permute-start(f32[2,16,8,128]{3,2,1,0:T(8,128)S(1)} %pad_maximum_fusion.3), channel_id=1, source_target_pairs={{32,0},{232,8},{48,16},{248,24},{64,32},{8,40},{80,48},{24,56},{96... | collective-permute-start | bytes 393224 | tf_op jit(solution)/shard_map/ppermute | solution.py:259
  24.9 1.6 %collective-permute-done.12 = f32[2,16,8,128]{3,2,1,0:T(8,128)S(1)} collective-permute-done((f32[2,16,8,128]{3,2,1,0:T(8,128)S(1)}, f32[2,16,8,128]{3,2,1,0:T(8,128)S(1)}, u32[]{:S(2)}, u32[]{:S(2)}) %collective-permute-start.12) | collective-permute-done | bytes 131104 | tf_op jit(solution)/shard_map/ppermute | solution.py:259
  26.5 0.6 %collective-permute-start.13 = (f32[2,16,8,128]{3,2,1,0:T(8,128)S(1)}, f32[2,16,8,128]{3,2,1,0:T(8,128)S(1)}, u32[]{:S(2)}, u32[]{:S(2)}) collective-permute-start(f32[2,16,8,128]{3,2,1,0:T(8,128)S(1)} %collective-permute-done.12), channel_id=1, source_target_pairs={{8,0},{0,8},{24,16},{16,24},{40,32},{32,40},{56,48},{48,56},{72,64... | collective-permute-start | bytes 393224 | tf_op jit(solution)/shard_map/ppermute | solution.py:259
  27.1 0.8 %collective-permute-done.7 = f32[2,16,8,128]{3,2,1,0:T(8,128)S(1)} collective-permute-done((f32[2,16,8,128]{3,2,1,0:T(8,128)S(1)}, f32[2,16,8,128]{3,2,1,0:T(8,128)S(1)}, u32[]{:S(2)}, u32[]{:S(2)}) %collective-permute-start.7) | collective-permute-done | bytes 131104 | tf_op jit(solution)/shard_map/ppermute | solution.py:259
  29.2 3.7 %collective-permute-start.16 = (f32[8,6,8,128]{3,2,1,0:T(8,128)S(1)}, f32[8,6,8,128]{3,2,1,0:T(8,128)S(1)}, u32[]{:S(2)}, u32[]{:S(2)}) collective-permute-start(f32[8,6,8,128]{3,2,1,0:T(8,128)S(1)} %get-tuple-element.44), channel_id=1, source_target_pairs={{0,1},{1,2},{2,3},{3,4},{4,5},{5,6},{6,7},{7,0},{8,9},{9,10},{10,1... | collective-permute-start | bytes 589832 | tf_op jit(solution)/shard_map/ppermute | solution.py:310
  32.9 2.2 %collective-permute-done.5.xr = f32[12,128,128]{2,1,0:T(8,128)S(1)} collective-permute-done((f32[12,128,128]{2,1,0:T(8,128)S(1)}, f32[12,128,128]{2,1,0:T(8,128)S(1)}, u32[]{:S(2)}, u32[]{:S(2)}) %collective-permute-start.5) | collective-permute-done | bytes 786464 | tf_op jit(solution)/shard_map/ppermute | solution.py:284
  35.2 0.7 %shard_map.48 = (f32[16,128,128]{2,1,0:T(8,128)S(1)}, f32[6,128,128]{2,1,0:T(8,128)S(1)}, f32[6,128,128]{2,1,0:T(8,128)S(1)}) custom-call(f32[16,128,128]{2,1,0:T(8,128)S(1)} %bitcast.28, f32[16,128,128]{2,1,0:T(8,128)S(1)} %shard_map.46.w1, f32[12,128,128]{2,1,0:T(8,128)S(1)} %collective-permute-done.4.xl, f32[12,128,128]{2,1,0:T(8,128)S(1)} %collective-permute-done.5.xr, ...), custom_call_target="tpu_custom_call" | custom-call | tf_op jit(solution)/shard_map/pallas_call | solution.py:240
  36.1 2.0 %collective-permute-start.15 = (f32[6,128,128]{2,1,0:T(8,128)S(1)}, f32[6,128,128]{2,1,0:T(8,128)S(1)}, u32[]{:S(2)}, u32[]{:S(2)}) collective-permute-start(f32[6,128,128]{2,1,0:T(8,128)S(1)} %get-tuple-element.32), channel_id=1, source_target_pairs={{1,0},{2,1},{3,2},{4,3},{5,4},{6,5},{7,6},{0,7},{9,8},{10,9},{11,1... | collective-permute-start | bytes 1179656 | tf_op jit(solution)/shard_map/ppermute | solution.py:313
  38.1 1.2 %collective-permute-done.17.ends_r = f32[8,6,8,128]{3,2,1,0:T(8,128)S(1)} collective-permute-done((f32[8,6,8,128]{3,2,1,0:T(8,128)S(1)}, f32[8,6,8,128]{3,2,1,0:T(8,128)S(1)}, u32[]{:S(2)}, u32[]{:S(2)}) %collective-permute-start.17) | collective-permute-done | bytes 196640 | tf_op jit(solution)/shard_map/ppermute | solution.py:310
  39.8 2.8 %shard_map.49 = (f32[12,128,128]{2,1,0:T(8,128)S(1)}, f32[16,128,128]{2,1,0:T(8,128)S(1)}) custom-call(f32[16,128,128]{2,1,0:T(8,128)S(1)} %bitcast.29, f32[12,128,128]{2,1,0:T(8,128)S(1)} %collective-permute-done.4.xl, f32[12,128,128]{2,1,0:T(8,128)S(1)} %collective-permute-done.5.xr, f32[16,128,128]{2,1,0:T(8,128)S(1)} %get-tuple-element.33.y1, ...), custom_call_target="tpu_custom_call" | custom-call | tf_op jit(solution)/shard_map/pallas_call | solution.py:240
  42.7 3.8 %shard_map.50 = (f32[6,128,128]{2,1,0:T(8,128)S(1)}, f32[6,128,128]{2,1,0:T(8,128)S(1)}, f32[16,128,128]{2,1,0:T(8,128)S(1)}) custom-call(f32[12,128,128]{2,1,0:T(8,128)S(1)} %collective-permute-done.4.xl, f32[12,128,128]{2,1,0:T(8,128)S(1)} %collective-permute-done.5.xr, f32[16,128,128]{2,1,0:T(8,128)S(1)} %get-tuple-element.33.y1, ...), custom_call_target="tpu_custom_call" | custom-call | tf_op jit(solution)/shard_map/pallas_call | solution.py:240
  46.5 1.0 %collective-permute-done.14.far_l = f32[6,128,128]{2,1,0:T(8,128)S(1)} collective-permute-done((f32[6,128,128]{2,1,0:T(8,128)S(1)}, f32[6,128,128]{2,1,0:T(8,128)S(1)}, u32[]{:S(2)}, u32[]{:S(2)}) %collective-permute-start.14) | collective-permute-done | bytes 393248 | tf_op jit(solution)/shard_map/ppermute | solution.py:314
  47.5 2.2 %collective-permute-done.15.far_r = f32[6,128,128]{2,1,0:T(8,128)S(1)} collective-permute-done((f32[6,128,128]{2,1,0:T(8,128)S(1)}, f32[6,128,128]{2,1,0:T(8,128)S(1)}, u32[]{:S(2)}, u32[]{:S(2)}) %collective-permute-start.15) | collective-permute-done | bytes 393248 | tf_op jit(solution)/shard_map/ppermute | solution.py:313
  49.7 1.4 %shard_map.51 = f32[16,128,128]{2,1,0:T(8,128)} custom-call(f32[6,128,128]{2,1,0:T(8,128)S(1)} %collective-permute-done.14.far_l, f32[6,128,128]{2,1,0:T(8,128)S(1)} %collective-permute-done.15.far_r, f32[6,128,128]{2,1,0:T(8,128)S(1)} %get-tuple-element.36.y2l, f32[6,128,128]{2,1,0:T(8,128)S(1)} %get-tuple-element.37.y2r, ...), custom_call_target="tpu_custom_call" | custom-call | flops 2621440 | bytes 2097152 | tf_op jit(solution)/shard_map/pallas_call | solution.py:326
  (53 shorter events, 3.3 us)
Async XLA Ops:
  0.0 13.7 %copy-start = (f32[1,16,128,128]{3,2,1,0:T(8,128)S(1)}, f32[1,16,128,128]{3,2,1,0:T(8,128)}, u32[]{:S(2)}) copy-start(f32[1,16,128,128]{3,2,1,0:T(8,128)} %param.4) | copy-start | bytes 3145732
  0.0 1.6 %collective-permute-start = (f32[16,4,128]{2,1,0:T(4,128)}, f32[16,4,128]{2,1,0:T(4,128)S(1)}, u32[]{:S(2)}, u32[]{:S(2)}) collective-permute-start(f32[16,4,128]{2,1,0:T(4,128)} %param.5), channel_id=1, source_target_pairs={{8,0},{0,8},{24,16},{16,24},{40,32},{32,40},{56,48},{48,56},{72,64... | collective-permute-start | bytes 98312 | tf_op jit(solution)/shard_map/ppermute | solution.py:259
  0.0 1.6 %copy-start.3 = (f32[16,4,128]{2,1,0:T(4,128)S(1)}, f32[16,4,128]{2,1,0:T(4,128)}, u32[]{:S(2)}) copy-start(f32[16,4,128]{2,1,0:T(4,128)} %param.5) | copy-start | bytes 98308
  1.6 12.1 %copy-start.2 = (bf16[256,256]{1,0:T(8,128)(2,1)S(1)}, bf16[256,256]{1,0:T(8,128)(2,1)}, u32[]{:S(2)}) copy-start(bf16[256,256]{1,0:T(8,128)(2,1)} %constant.24.clone.right) | copy-start | bytes 393220
  1.6 12.1 %copy-start.1 = (bf16[256,256]{1,0:T(8,128)(2,1)S(1)}, bf16[256,256]{1,0:T(8,128)(2,1)}, u32[]{:S(2)}) copy-start(bf16[256,256]{1,0:T(8,128)(2,1)} %constant.25.clone.left) | copy-start | bytes 393220
  1.7 14.8 %collective-permute-start.2 = (f32[16,8,128]{2,1,0:T(8,128)S(1)}, f32[16,8,128]{2,1,0:T(8,128)S(1)}, u32[]{:S(2)}, u32[]{:S(2)}) collective-permute-start(f32[16,8,128]{2,1,0:T(8,128)S(1)} %maximum_select_fusion), channel_id=1, source_target_pairs={{112,0},{184,8},{96,16},{168,24},{144,32},{216,40},{128,48},{200,5... | collective-permute-start | bytes 196616 | tf_op jit(solution)/shard_map/ppermute | solution.py:259
  11.0 6.2 %collective-permute-start.1 = (f32[16,8,128]{2,1,0:T(8,128)S(1)}, f32[16,8,128]{2,1,0:T(8,128)S(1)}, u32[]{:S(2)}, u32[]{:S(2)}) collective-permute-start(f32[16,8,128]{2,1,0:T(8,128)S(1)} %maximum_select_fusion), channel_id=1, source_target_pairs={{96,0},{168,8},{112,16},{184,24},{128,32},{200,40},{144,48},{216,5... | collective-permute-start | bytes 196616 | tf_op jit(solution)/shard_map/ppermute | solution.py:259
  11.1 5.4 %collective-permute-start.3 = (f32[8,8,128]{2,1,0:T(8,128)S(1)}, f32[8,8,128]{2,1,0:T(8,128)S(1)}, u32[]{:S(2)}, u32[]{:S(2)}) collective-permute-start(f32[8,8,128]{2,1,0:T(8,128)S(1)} %slice_select_fusion.1), channel_id=1, source_target_pairs={{16,0},{24,8},{0,16},{8,24},{48,32},{56,40},{32,48},{40,56},{80,64... | collective-permute-start | bytes 98312 | tf_op jit(solution)/shard_map/ppermute | solution.py:259
  11.6 21.3 %collective-permute-start.4 = (f32[12,128,128]{2,1,0:T(8,128)S(1)}, f32[12,128,128]{2,1,0:T(8,128)S(1)}, u32[]{:S(2)}, u32[]{:S(2)}) collective-permute-start(f32[12,128,128]{2,1,0:T(8,128)S(1)} %get-tuple-element.25), channel_id=1, source_target_pairs={{0,1},{1,2},{2,3},{3,4},{4,5},{5,6},{6,7},{7,0},{8,9},{9,10},{10,1... | collective-permute-start | bytes 2359304 | tf_op jit(solution)/shard_map/ppermute | solution.py:283
  12.7 22.4 %collective-permute-start.5 = (f32[12,128,128]{2,1,0:T(8,128)S(1)}, f32[12,128,128]{2,1,0:T(8,128)S(1)}, u32[]{:S(2)}, u32[]{:S(2)}) collective-permute-start(f32[12,128,128]{2,1,0:T(8,128)S(1)} %get-tuple-element.26), channel_id=1, source_target_pairs={{1,0},{2,1},{3,2},{4,3},{5,4},{6,5},{7,6},{0,7},{9,8},{10,9},{11,1... | collective-permute-start | bytes 2359304 | tf_op jit(solution)/shard_map/ppermute | solution.py:284
  17.2 3.2 %collective-permute-start.6 = (f32[24,8,128]{2,1,0:T(8,128)S(1)}, f32[24,8,128]{2,1,0:T(8,128)S(1)}, u32[]{:S(2)}, u32[]{:S(2)}) collective-permute-start(f32[24,8,128]{2,1,0:T(8,128)S(1)} %slice.60), channel_id=1, source_target_pairs={{8,0},{0,8},{24,16},{16,24},{40,32},{32,40},{56,48},{48,56},{72,64... | collective-permute-start | bytes 294920 | tf_op jit(solution)/shard_map/ppermute | solution.py:259
  17.4 7.4 %collective-permute-start.9 = (f32[2,16,8,128]{3,2,1,0:T(8,128)S(1)}, f32[2,16,8,128]{3,2,1,0:T(8,128)S(1)}, u32[]{:S(2)}, u32[]{:S(2)}) collective-permute-start(f32[2,16,8,128]{3,2,1,0:T(8,128)S(1)} %pad_maximum_fusion.4), channel_id=1, source_target_pairs={{32,0},{232,8},{48,16},{248,24},{64,32},{8,40},{80,48},{24,56},{96... | collective-permute-start | bytes 393224 | tf_op jit(solution)/shard_map/ppermute | solution.py:259
  20.2 1.3 %collective-permute-start.11 = (f32[16,8,128]{2,1,0:T(8,128)S(1)}, f32[16,8,128]{2,1,0:T(8,128)S(1)}, u32[]{:S(2)}, u32[]{:S(2)}) collective-permute-start(f32[16,8,128]{2,1,0:T(8,128)S(1)} %slice.62), channel_id=1, source_target_pairs={{8,0},{0,8},{24,16},{16,24},{40,32},{32,40},{56,48},{48,56},{72,64... | collective-permute-start | bytes 196616 | tf_op jit(solution)/shard_map/ppermute | solution.py:259
  21.5 5.0 %collective-permute-start.12 = (f32[2,16,8,128]{3,2,1,0:T(8,128)S(1)}, f32[2,16,8,128]{3,2,1,0:T(8,128)S(1)}, u32[]{:S(2)}, u32[]{:S(2)}) collective-permute-start(f32[2,16,8,128]{3,2,1,0:T(8,128)S(1)} %pad_maximum_fusion.5), channel_id=1, source_target_pairs={{32,0},{232,8},{48,16},{248,24},{64,32},{8,40},{80,48},{24,56},{96... | collective-permute-start | bytes 393224 | tf_op jit(solution)/shard_map/ppermute | solution.py:259
  22.8 5.2 %collective-permute-start.7 = (f32[2,16,8,128]{3,2,1,0:T(8,128)S(1)}, f32[2,16,8,128]{3,2,1,0:T(8,128)S(1)}, u32[]{:S(2)}, u32[]{:S(2)}) collective-permute-start(f32[2,16,8,128]{3,2,1,0:T(8,128)S(1)} %pad_maximum_fusion.3), channel_id=1, source_target_pairs={{32,0},{232,8},{48,16},{248,24},{64,32},{8,40},{80,48},{24,56},{96... | collective-permute-start | bytes 393224 | tf_op jit(solution)/shard_map/ppermute | solution.py:259
  24.8 3.8 %collective-permute-start.10 = (f32[2,16,8,128]{3,2,1,0:T(8,128)S(1)}, f32[2,16,8,128]{3,2,1,0:T(8,128)S(1)}, u32[]{:S(2)}, u32[]{:S(2)}) collective-permute-start(f32[2,16,8,128]{3,2,1,0:T(8,128)S(1)} %collective-permute-done.9), channel_id=1, source_target_pairs={{8,0},{0,8},{24,16},{16,24},{40,32},{32,40},{56,48},{48,56},{72,64... | collective-permute-start | bytes 393224 | tf_op jit(solution)/shard_map/ppermute | solution.py:259
  26.5 2.6 %collective-permute-start.13 = (f32[2,16,8,128]{3,2,1,0:T(8,128)S(1)}, f32[2,16,8,128]{3,2,1,0:T(8,128)S(1)}, u32[]{:S(2)}, u32[]{:S(2)}) collective-permute-start(f32[2,16,8,128]{3,2,1,0:T(8,128)S(1)} %collective-permute-done.12), channel_id=1, source_target_pairs={{8,0},{0,8},{24,16},{16,24},{40,32},{32,40},{56,48},{48,56},{72,64... | collective-permute-start | bytes 393224 | tf_op jit(solution)/shard_map/ppermute | solution.py:259
  27.9 4.9 %collective-permute-start.8 = (f32[2,16,8,128]{3,2,1,0:T(8,128)S(1)}, f32[2,16,8,128]{3,2,1,0:T(8,128)S(1)}, u32[]{:S(2)}, u32[]{:S(2)}) collective-permute-start(f32[2,16,8,128]{3,2,1,0:T(8,128)S(1)} %collective-permute-done.7), channel_id=1, source_target_pairs={{8,0},{0,8},{24,16},{16,24},{40,32},{32,40},{56,48},{48,56},{72,64... | collective-permute-start | bytes 393224 | tf_op jit(solution)/shard_map/ppermute | solution.py:259
  28.6 10.7 %collective-permute-start.17 = (f32[8,6,8,128]{3,2,1,0:T(8,128)S(1)}, f32[8,6,8,128]{3,2,1,0:T(8,128)S(1)}, u32[]{:S(2)}, u32[]{:S(2)}) collective-permute-start(f32[8,6,8,128]{3,2,1,0:T(8,128)S(1)} %get-tuple-element.43), channel_id=1, source_target_pairs={{1,0},{2,1},{3,2},{4,3},{5,4},{6,5},{7,6},{0,7},{9,8},{10,9},{11,1... | collective-permute-start | bytes 589832 | tf_op jit(solution)/shard_map/ppermute | solution.py:310
  29.2 10.3 %collective-permute-start.16 = (f32[8,6,8,128]{3,2,1,0:T(8,128)S(1)}, f32[8,6,8,128]{3,2,1,0:T(8,128)S(1)}, u32[]{:S(2)}, u32[]{:S(2)}) collective-permute-start(f32[8,6,8,128]{3,2,1,0:T(8,128)S(1)} %get-tuple-element.44), channel_id=1, source_target_pairs={{0,1},{1,2},{2,3},{3,4},{4,5},{5,6},{6,7},{7,0},{8,9},{9,10},{10,1... | collective-permute-start | bytes 589832 | tf_op jit(solution)/shard_map/ppermute | solution.py:310
  36.0 11.5 %collective-permute-start.14 = (f32[6,128,128]{2,1,0:T(8,128)S(1)}, f32[6,128,128]{2,1,0:T(8,128)S(1)}, u32[]{:S(2)}, u32[]{:S(2)}) collective-permute-start(f32[6,128,128]{2,1,0:T(8,128)S(1)} %get-tuple-element.31), channel_id=1, source_target_pairs={{0,1},{1,2},{2,3},{3,4},{4,5},{5,6},{6,7},{7,0},{8,9},{9,10},{10,1... | collective-permute-start | bytes 1179656 | tf_op jit(solution)/shard_map/ppermute | solution.py:314
  36.1 13.6 %collective-permute-start.15 = (f32[6,128,128]{2,1,0:T(8,128)S(1)}, f32[6,128,128]{2,1,0:T(8,128)S(1)}, u32[]{:S(2)}, u32[]{:S(2)}) collective-permute-start(f32[6,128,128]{2,1,0:T(8,128)S(1)} %get-tuple-element.32), channel_id=1, source_target_pairs={{1,0},{2,1},{3,2},{4,3},{5,4},{6,5},{7,6},{0,7},{9,8},{10,9},{11,1... | collective-permute-start | bytes 1179656 | tf_op jit(solution)/shard_map/ppermute | solution.py:313
  39.3 3.3 %collective-permute-start.19 = (f32[8,6,8,128]{3,2,1,0:T(8,128)S(1)}, f32[8,6,8,128]{3,2,1,0:T(8,128)S(1)}, u32[]{:S(2)}, u32[]{:S(2)}) collective-permute-start(f32[8,6,8,128]{3,2,1,0:T(8,128)S(1)} %collective-permute-done.17.ends_r), channel_id=1, source_target_pairs={{8,0},{0,8},{24,16},{16,24},{40,32},{32,40},{56,48},{48,56},{72,64... | collective-permute-start | bytes 589832 | tf_op jit(solution)/shard_map/ppermute | solution.py:259
  39.5 3.2 %collective-permute-start.18 = (f32[8,6,8,128]{3,2,1,0:T(8,128)S(1)}, f32[8,6,8,128]{3,2,1,0:T(8,128)S(1)}, u32[]{:S(2)}, u32[]{:S(2)}) collective-permute-start(f32[8,6,8,128]{3,2,1,0:T(8,128)S(1)} %collective-permute-done.16.ends_l), channel_id=1, source_target_pairs={{8,0},{0,8},{24,16},{16,24},{40,32},{32,40},{56,48},{48,56},{72,64... | collective-permute-start | bytes 589832 | tf_op jit(solution)/shard_map/ppermute | solution.py:259

commit v4 on v3

--- a/solution.py
+++ b/solution.py
@@ -94,11 +94,12 @@
 
 
 def kernel_place(mine, got, others, vown):
-    way = 1 - 2 * (lax.axis_index("band") % 2)
-    for ref, shift, turn in ((mine, 0, 1), (got, 1, 1), (others, -1, -1)):
-        for i, (dz, dh) in enumerate(SLOTS):
-            if shift + turn * dz != -4:
-                place(ref, i, shift + turn * dz, dh, way, vown, 0, 16)
+    core = lax.axis_index("band") % 2
+    for i, (steps, dh) in enumerate(SLOTS):
+        place(mine, i, steps, dh, 1 - 2 * core, vown, 0, 16)
+    for ref, c in ((got, core), (others, 1 - core)):
+        for i, (steps, dh) in enumerate(END_SLOTS[3:]):
+            place(ref, i, steps, c if dh is None else dh, 1 - 2 * c, vown, 0, 16)
 
 
 def kernel_own(x, left, right, w1, flat):
@@ -289,7 +290,8 @@
     mine = jnp.stack(
         [block, in_order(part, twins[32:], 0), along, across, twins[:16], twins[16:32]], 0
     )
-    gots = [of_band(mine[i : i + 2], lambda z, h, c: at(z + 1 - 2 * c, h, c)) for i in range(0, 6, 2)]
+    half = jnp.where(core0, mine[2:3], mine[3:4])
+    gots = [of_band(part, lambda z, h, c: at(z + 1 - 2 * c, h, c)) for part in (mine[:2], jnp.concatenate([half, mine[4:]], 0))]
     got = jnp.concatenate(gots, 0)
     others = jnp.concatenate([flip(g) for g in gots], 0)
     xl, xr, others = lax.optimization_barrier((xl, xr, others))
@@ -301,9 +303,9 @@
             mine[3],
             got[0],
             got[1],
-            jnp.where(core0, got[2], got[3]),
+            got[2],
+            got[3],
             got[4],
-            got[5],
         ],
         0,
     )

time: 51.4 us -> 51.5 us (level)
  waiting for transfers between devices: 12.2 us -> 14.8 us
  starting transfers between devices: 26.5 us -> 24.1 us
    ppermute x14 -> x12, starting transfers between devices: 18.1 us -> 15.6 us  [of_band(): lax.ppermute(value, 'band', [(source(i // 4, i // 2 % 2, i % 2), i) for i...]
    ppermute x14 -> x12, waiting for transfers between devices: 5.57 us -> 6.89 us  [of_band(): lax.ppermute(value, 'band', [(source(i // 4, i // 2 % 2, i % 2), i) for i...]
    ppermute x1, waiting for transfers between devices: 2.22 us -> 3.3 us  [shards(): xr = lax.ppermute(first, 'slab', down)]
  transfers between devices with their start and end apart: 20 -> 18, of which waited for: 9 -> 8; matrix products, arithmetic and copies ran while one was open for 4% -> 4% of each run, Pallas kernels for 17% -> 17%
where the time goes in v4:
time: 51.5 us; the launch traced here: 51.4 us
  starting transfers between devices  24.1 us (47%)
  waiting for transfers between devices  14.8 us (29%)
  Pallas kernels  10.2 us (20%)
  local copies, waits for them, and re-layouts  1.71 us (3%)
    ppermute x12, starting transfers between devices, of_band(): lax.ppermute(value, 'band', [(source(i // 4, i // 2 % 2, i % 2), i) for i...  15.6 us
    pallas_call x5, Pallas kernels, call(): pl.pallas_call(body, out_shape=tuple((jax.ShapeDtypeStruct(o, F32) for o...  8.82 us
    ppermute x12, waiting for transfers between devices, of_band(): lax.ppermute(value, 'band', [(source(i // 4, i // 2 % 2, i % 2), i) for i...  6.89 us
    ppermute x1, starting transfers between devices, shards(): lax.ppermute(ends[:, nx - W:], 'slab', up)  3.47 us
    ppermute x1, waiting for transfers between devices, shards(): xr = lax.ppermute(first, 'slab', down)  3.3 us
    ppermute x1, waiting for transfers between devices, shards(): far_r = lax.ppermute(to_left, 'slab', down)  2.38 us
    ppermute x1, starting transfers between devices, shards(): far_r = lax.ppermute(to_left, 'slab', down)  2.04 us
    slice x1, local copies, waits for them, and re-layouts, shards(): x[:12]  1.57 us
  transfers between devices with their start and end apart: 18, of which 8 were waited for; matrix products, arithmetic and copies ran while one was open for 4% of the time, Pallas kernels for 17%

profile of v4, /device:TPU:24, one launch (start us, length us, event | category | flops | bytes accessed | tf_op | source)
XLA Modules:
  0.0 51.4 jit_solution(18439063366706771449)
XLA Ops:
  0.0 1.6 %slice_bitcast_fusion = (f32[12,128,128]{2,1,0:T(8,128)S(1)}, f32[12,128,128]{2,1,0:T(8,128)S(1)}) fusion(f32[1,16,128,128]{3,2,1,0:T(8,128)} %param.4), kind=kLoop, calls=%fused_computation | loop fusion | bytes 3145728 | tf_op jit(solution)/shard_map/slice | solution.py:280
  1.7 9.3 %collective-permute-start.2 = (f32[16,8,128]{2,1,0:T(8,128)S(1)}, f32[16,8,128]{2,1,0:T(8,128)S(1)}, u32[]{:S(2)}, u32[]{:S(2)}) collective-permute-start(f32[16,8,128]{2,1,0:T(8,128)S(1)} %maximum_select_fusion), channel_id=1, source_target_pairs={{112,0},{184,8},{96,16},{168,24},{144,32},{216,40},{128,48},{200,5... | collective-permute-start | bytes 196616 | tf_op jit(solution)/shard_map/ppermute | solution.py:260
  11.1 0.6 %collective-permute-start.3 = (f32[8,8,128]{2,1,0:T(8,128)S(1)}, f32[8,8,128]{2,1,0:T(8,128)S(1)}, u32[]{:S(2)}, u32[]{:S(2)}) collective-permute-start(f32[8,8,128]{2,1,0:T(8,128)S(1)} %slice_select_fusion), channel_id=1, source_target_pairs={{16,0},{24,8},{0,16},{8,24},{48,32},{56,40},{32,48},{40,56},{80,64... | collective-permute-start | bytes 98312 | tf_op jit(solution)/shard_map/ppermute | solution.py:260
  11.6 1.1 %collective-permute-start.4 = (f32[12,128,128]{2,1,0:T(8,128)S(1)}, f32[12,128,128]{2,1,0:T(8,128)S(1)}, u32[]{:S(2)}, u32[]{:S(2)}) collective-permute-start(f32[12,128,128]{2,1,0:T(8,128)S(1)} %get-tuple-element.25), channel_id=1, source_target_pairs={{0,1},{1,2},{2,3},{3,4},{4,5},{5,6},{6,7},{7,0},{8,9},{9,10},{10,1... | collective-permute-start | bytes 2359304 | tf_op jit(solution)/shard_map/ppermute | solution.py:284
  12.7 0.9 %collective-permute-start.5 = (f32[12,128,128]{2,1,0:T(8,128)S(1)}, f32[12,128,128]{2,1,0:T(8,128)S(1)}, u32[]{:S(2)}, u32[]{:S(2)}) collective-permute-start(f32[12,128,128]{2,1,0:T(8,128)S(1)} %get-tuple-element.26), channel_id=1, source_target_pairs={{1,0},{2,1},{3,2},{4,3},{5,4},{6,5},{7,6},{0,7},{9,8},{10,9},{11,1... | collective-permute-start | bytes 2359304 | tf_op jit(solution)/shard_map/ppermute | solution.py:285
  13.7 1.4 %shard_map.46.w1 = f32[16,128,128]{2,1,0:T(8,128)S(1)} custom-call(f32[16,128,128]{2,1,0:T(8,128)S(1)} %bitcast.29, bf16[256,256]{1,0:T(8,128)(2,1)S(1)} %copy-done.1, bf16[256,256]{1,0:T(8,128)(2,1)S(1)} %copy-done.2), custom_call_target="tpu_custom_call" | custom-call | flops 5242880000 | bytes 2359296 | tf_op jit(solution)/shard_map/pallas_call | solution.py:241
  15.1 1.4 %collective-permute-done.3 = f32[8,8,128]{2,1,0:T(8,128)S(1)} collective-permute-done((f32[8,8,128]{2,1,0:T(8,128)S(1)}, f32[8,8,128]{2,1,0:T(8,128)S(1)}, u32[]{:S(2)}, u32[]{:S(2)}) %collective-permute-start.3) | collective-permute-done | bytes 32800 | tf_op jit(solution)/shard_map/ppermute | solution.py:260
  16.5 0.6 %collective-permute-done.1 = f32[16,8,128]{2,1,0:T(8,128)S(1)} collective-permute-done((f32[16,8,128]{2,1,0:T(8,128)S(1)}, f32[16,8,128]{2,1,0:T(8,128)S(1)}, u32[]{:S(2)}, u32[]{:S(2)}) %collective-permute-start.1) | collective-permute-done | bytes 65568 | tf_op jit(solution)/shard_map/ppermute | solution.py:260
  17.8 0.9 %collective-permute-done.6 = f32[24,8,128]{2,1,0:T(8,128)S(1)} collective-permute-done((f32[24,8,128]{2,1,0:T(8,128)S(1)}, f32[24,8,128]{2,1,0:T(8,128)S(1)}, u32[]{:S(2)}, u32[]{:S(2)}) %collective-permute-start.6) | collective-permute-done | bytes 98336 | tf_op jit(solution)/shard_map/ppermute | solution.py:260
  18.8 2.9 %collective-permute-start.10 = (f32[3,16,8,128]{3,2,1,0:T(8,128)S(1)}, f32[3,16,8,128]{3,2,1,0:T(8,128)S(1)}, u32[]{:S(2)}, u32[]{:S(2)}) collective-permute-start(f32[3,16,8,128]{3,2,1,0:T(8,128)S(1)} %pad_maximum_fusion.2), channel_id=1, source_target_pairs={{32,0},{232,8},{48,16},{248,24},{64,32},{8,40},{80,48},{24,56},{96... | collective-permute-start | bytes 589832 | tf_op jit(solution)/shard_map/ppermute | solution.py:260
  21.7 1.1 %collective-permute-start.7 = (f32[2,16,8,128]{3,2,1,0:T(8,128)S(1)}, f32[2,16,8,128]{3,2,1,0:T(8,128)S(1)}, u32[]{:S(2)}, u32[]{:S(2)}) collective-permute-start(f32[2,16,8,128]{3,2,1,0:T(8,128)S(1)} %pad_maximum_fusion.4), channel_id=1, source_target_pairs={{32,0},{232,8},{48,16},{248,24},{64,32},{8,40},{80,48},{24,56},{96... | collective-permute-start | bytes 393224 | tf_op jit(solution)/shard_map/ppermute | solution.py:260
  22.9 3.9 %collective-permute-done.7 = f32[2,16,8,128]{3,2,1,0:T(8,128)S(1)} collective-permute-done((f32[2,16,8,128]{3,2,1,0:T(8,128)S(1)}, f32[2,16,8,128]{3,2,1,0:T(8,128)S(1)}, u32[]{:S(2)}, u32[]{:S(2)}) %collective-permute-start.7) | collective-permute-done | bytes 131104 | tf_op jit(solution)/shard_map/ppermute | solution.py:260
  26.8 0.4 collective-permute-start.8
  27.4 0.8 %collective-permute-start.15 = (f32[8,6,8,128]{3,2,1,0:T(8,128)S(1)}, f32[8,6,8,128]{3,2,1,0:T(8,128)S(1)}, u32[]{:S(2)}, u32[]{:S(2)}) collective-permute-start(f32[8,6,8,128]{3,2,1,0:T(8,128)S(1)} %get-tuple-element.43), channel_id=1, source_target_pairs={{1,0},{2,1},{3,2},{4,3},{5,4},{6,5},{7,6},{0,7},{9,8},{10,9},{11,1... | collective-permute-start | bytes 589832 | tf_op jit(solution)/shard_map/ppermute | solution.py:312
  28.3 3.5 %collective-permute-start.14 = (f32[8,6,8,128]{3,2,1,0:T(8,128)S(1)}, f32[8,6,8,128]{3,2,1,0:T(8,128)S(1)}, u32[]{:S(2)}, u32[]{:S(2)}) collective-permute-start(f32[8,6,8,128]{3,2,1,0:T(8,128)S(1)} %get-tuple-element.44), channel_id=1, source_target_pairs={{0,1},{1,2},{2,3},{3,4},{4,5},{5,6},{6,7},{7,0},{8,9},{9,10},{10,1... | collective-permute-start | bytes 589832 | tf_op jit(solution)/shard_map/ppermute | solution.py:312
  31.8 3.3 %collective-permute-done.5.xr = f32[12,128,128]{2,1,0:T(8,128)S(1)} collective-permute-done((f32[12,128,128]{2,1,0:T(8,128)S(1)}, f32[12,128,128]{2,1,0:T(8,128)S(1)}, u32[]{:S(2)}, u32[]{:S(2)}) %collective-permute-start.5) | collective-permute-done | bytes 786464 | tf_op jit(solution)/shard_map/ppermute | solution.py:285
  35.2 0.7 %shard_map.48 = (f32[16,128,128]{2,1,0:T(8,128)S(1)}, f32[6,128,128]{2,1,0:T(8,128)S(1)}, f32[6,128,128]{2,1,0:T(8,128)S(1)}) custom-call(f32[16,128,128]{2,1,0:T(8,128)S(1)} %bitcast.30, f32[16,128,128]{2,1,0:T(8,128)S(1)} %shard_map.46.w1, f32[12,128,128]{2,1,0:T(8,128)S(1)} %collective-permute-done.4.xl, f32[12,128,128]{2,1,0:T(8,128)S(1)} %collective-permute-done.5.xr, ...), custom_call_target="tpu_custom_call" | custom-call | tf_op jit(solution)/shard_map/pallas_call | solution.py:241
  36.1 2.0 %collective-permute-start.13 = (f32[6,128,128]{2,1,0:T(8,128)S(1)}, f32[6,128,128]{2,1,0:T(8,128)S(1)}, u32[]{:S(2)}, u32[]{:S(2)}) collective-permute-start(f32[6,128,128]{2,1,0:T(8,128)S(1)} %get-tuple-element.32), channel_id=1, source_target_pairs={{1,0},{2,1},{3,2},{4,3},{5,4},{6,5},{7,6},{0,7},{9,8},{10,9},{11,1... | collective-permute-start | bytes 1179656 | tf_op jit(solution)/shard_map/ppermute | solution.py:315
  38.1 1.2 %collective-permute-done.15.ends_r = f32[8,6,8,128]{3,2,1,0:T(8,128)S(1)} collective-permute-done((f32[8,6,8,128]{3,2,1,0:T(8,128)S(1)}, f32[8,6,8,128]{3,2,1,0:T(8,128)S(1)}, u32[]{:S(2)}, u32[]{:S(2)}) %collective-permute-start.15) | collective-permute-done | bytes 196640 | tf_op jit(solution)/shard_map/ppermute | solution.py:312
  39.8 2.8 %shard_map.49 = (f32[12,128,128]{2,1,0:T(8,128)S(1)}, f32[16,128,128]{2,1,0:T(8,128)S(1)}) custom-call(f32[16,128,128]{2,1,0:T(8,128)S(1)} %bitcast.31, f32[12,128,128]{2,1,0:T(8,128)S(1)} %collective-permute-done.4.xl, f32[12,128,128]{2,1,0:T(8,128)S(1)} %collective-permute-done.5.xr, f32[16,128,128]{2,1,0:T(8,128)S(1)} %get-tuple-element.33.y1, ...), custom_call_target="tpu_custom_call" | custom-call | tf_op jit(solution)/shard_map/pallas_call | solution.py:241
  42.7 3.8 %shard_map.50 = (f32[6,128,128]{2,1,0:T(8,128)S(1)}, f32[6,128,128]{2,1,0:T(8,128)S(1)}, f32[16,128,128]{2,1,0:T(8,128)S(1)}) custom-call(f32[12,128,128]{2,1,0:T(8,128)S(1)} %collective-permute-done.4.xl, f32[12,128,128]{2,1,0:T(8,128)S(1)} %collective-permute-done.5.xr, f32[16,128,128]{2,1,0:T(8,128)S(1)} %get-tuple-element.33.y1, ...), custom_call_target="tpu_custom_call" | custom-call | tf_op jit(solution)/shard_map/pallas_call | solution.py:241
  46.5 1.0 %collective-permute-done.12.far_l = f32[6,128,128]{2,1,0:T(8,128)S(1)} collective-permute-done((f32[6,128,128]{2,1,0:T(8,128)S(1)}, f32[6,128,128]{2,1,0:T(8,128)S(1)}, u32[]{:S(2)}, u32[]{:S(2)}) %collective-permute-start.12) | collective-permute-done | bytes 393248 | tf_op jit(solution)/shard_map/ppermute | solution.py:316
  47.5 2.4 %collective-permute-done.13.far_r = f32[6,128,128]{2,1,0:T(8,128)S(1)} collective-permute-done((f32[6,128,128]{2,1,0:T(8,128)S(1)}, f32[6,128,128]{2,1,0:T(8,128)S(1)}, u32[]{:S(2)}, u32[]{:S(2)}) %collective-permute-start.13) | collective-permute-done | bytes 393248 | tf_op jit(solution)/shard_map/ppermute | solution.py:315
  49.8 1.4 %shard_map.51 = f32[16,128,128]{2,1,0:T(8,128)} custom-call(f32[6,128,128]{2,1,0:T(8,128)S(1)} %collective-permute-done.12.far_l, f32[6,128,128]{2,1,0:T(8,128)S(1)} %collective-permute-done.13.far_r, f32[6,128,128]{2,1,0:T(8,128)S(1)} %get-tuple-element.36.y2l, f32[6,128,128]{2,1,0:T(8,128)S(1)} %get-tuple-element.37.y2r, ...), custom_call_target="tpu_custom_call" | custom-call | flops 2621440 | bytes 2097152 | tf_op jit(solution)/shard_map/pallas_call | solution.py:328
  (48 shorter events, 1.9 us)
Async XLA Ops:
  0.0 13.7 %copy-start = (f32[1,16,128,128]{3,2,1,0:T(8,128)S(1)}, f32[1,16,128,128]{3,2,1,0:T(8,128)}, u32[]{:S(2)}) copy-start(f32[1,16,128,128]{3,2,1,0:T(8,128)} %param.4) | copy-start | bytes 3145732
  0.0 1.6 %collective-permute-start = (f32[16,4,128]{2,1,0:T(4,128)}, f32[16,4,128]{2,1,0:T(4,128)S(1)}, u32[]{:S(2)}, u32[]{:S(2)}) collective-permute-start(f32[16,4,128]{2,1,0:T(4,128)} %param.5), channel_id=1, source_target_pairs={{8,0},{0,8},{24,16},{16,24},{40,32},{32,40},{56,48},{48,56},{72,64... | collective-permute-start | bytes 98312 | tf_op jit(solution)/shard_map/ppermute | solution.py:260
  0.0 1.6 %copy-start.3 = (f32[16,4,128]{2,1,0:T(4,128)S(1)}, f32[16,4,128]{2,1,0:T(4,128)}, u32[]{:S(2)}) copy-start(f32[16,4,128]{2,1,0:T(4,128)} %param.5) | copy-start | bytes 98308
  1.6 12.1 %copy-start.2 = (bf16[256,256]{1,0:T(8,128)(2,1)S(1)}, bf16[256,256]{1,0:T(8,128)(2,1)}, u32[]{:S(2)}) copy-start(bf16[256,256]{1,0:T(8,128)(2,1)} %constant.24.clone.right) | copy-start | bytes 393220
  1.6 12.1 %copy-start.1 = (bf16[256,256]{1,0:T(8,128)(2,1)S(1)}, bf16[256,256]{1,0:T(8,128)(2,1)}, u32[]{:S(2)}) copy-start(bf16[256,256]{1,0:T(8,128)(2,1)} %constant.25.clone.left) | copy-start | bytes 393220
  1.7 14.8 %collective-permute-start.2 = (f32[16,8,128]{2,1,0:T(8,128)S(1)}, f32[16,8,128]{2,1,0:T(8,128)S(1)}, u32[]{:S(2)}, u32[]{:S(2)}) collective-permute-start(f32[16,8,128]{2,1,0:T(8,128)S(1)} %maximum_select_fusion), channel_id=1, source_target_pairs={{112,0},{184,8},{96,16},{168,24},{144,32},{216,40},{128,48},{200,5... | collective-permute-start | bytes 196616 | tf_op jit(solution)/shard_map/ppermute | solution.py:260
  11.0 6.2 %collective-permute-start.1 = (f32[16,8,128]{2,1,0:T(8,128)S(1)}, f32[16,8,128]{2,1,0:T(8,128)S(1)}, u32[]{:S(2)}, u32[]{:S(2)}) collective-permute-start(f32[16,8,128]{2,1,0:T(8,128)S(1)} %maximum_select_fusion), channel_id=1, source_target_pairs={{96,0},{168,8},{112,16},{184,24},{128,32},{200,40},{144,48},{216,5... | collective-permute-start | bytes 196616 | tf_op jit(solution)/shard_map/ppermute | solution.py:260
  11.1 5.4 %collective-permute-start.3 = (f32[8,8,128]{2,1,0:T(8,128)S(1)}, f32[8,8,128]{2,1,0:T(8,128)S(1)}, u32[]{:S(2)}, u32[]{:S(2)}) collective-permute-start(f32[8,8,128]{2,1,0:T(8,128)S(1)} %slice_select_fusion), channel_id=1, source_target_pairs={{16,0},{24,8},{0,16},{8,24},{48,32},{56,40},{32,48},{40,56},{80,64... | collective-permute-start | bytes 98312 | tf_op jit(solution)/shard_map/ppermute | solution.py:260
  11.6 20.2 %collective-permute-start.4 = (f32[12,128,128]{2,1,0:T(8,128)S(1)}, f32[12,128,128]{2,1,0:T(8,128)S(1)}, u32[]{:S(2)}, u32[]{:S(2)}) collective-permute-start(f32[12,128,128]{2,1,0:T(8,128)S(1)} %get-tuple-element.25), channel_id=1, source_target_pairs={{0,1},{1,2},{2,3},{3,4},{4,5},{5,6},{6,7},{7,0},{8,9},{9,10},{10,1... | collective-permute-start | bytes 2359304 | tf_op jit(solution)/shard_map/ppermute | solution.py:284
  12.7 22.4 %collective-permute-start.5 = (f32[12,128,128]{2,1,0:T(8,128)S(1)}, f32[12,128,128]{2,1,0:T(8,128)S(1)}, u32[]{:S(2)}, u32[]{:S(2)}) collective-permute-start(f32[12,128,128]{2,1,0:T(8,128)S(1)} %get-tuple-element.26), channel_id=1, source_target_pairs={{1,0},{2,1},{3,2},{4,3},{5,4},{6,5},{7,6},{0,7},{9,8},{10,9},{11,1... | collective-permute-start | bytes 2359304 | tf_op jit(solution)/shard_map/ppermute | solution.py:285
  17.2 1.6 %collective-permute-start.9 = (f32[16,8,128]{2,1,0:T(8,128)S(1)}, f32[16,8,128]{2,1,0:T(8,128)S(1)}, u32[]{:S(2)}, u32[]{:S(2)}) collective-permute-start(f32[16,8,128]{2,1,0:T(8,128)S(1)} %slice.55), channel_id=1, source_target_pairs={{8,0},{0,8},{24,16},{16,24},{40,32},{32,40},{56,48},{48,56},{72,64... | collective-permute-start | bytes 196616 | tf_op jit(solution)/shard_map/ppermute | solution.py:260
  17.4 1.4 %collective-permute-start.6 = (f32[24,8,128]{2,1,0:T(8,128)S(1)}, f32[24,8,128]{2,1,0:T(8,128)S(1)}, u32[]{:S(2)}, u32[]{:S(2)}) collective-permute-start(f32[24,8,128]{2,1,0:T(8,128)S(1)} %slice.53), channel_id=1, source_target_pairs={{8,0},{0,8},{24,16},{16,24},{40,32},{32,40},{56,48},{48,56},{72,64... | collective-permute-start | bytes 294920 | tf_op jit(solution)/shard_map/ppermute | solution.py:260
  18.8 8.5 %collective-permute-start.10 = (f32[3,16,8,128]{3,2,1,0:T(8,128)S(1)}, f32[3,16,8,128]{3,2,1,0:T(8,128)S(1)}, u32[]{:S(2)}, u32[]{:S(2)}) collective-permute-start(f32[3,16,8,128]{3,2,1,0:T(8,128)S(1)} %pad_maximum_fusion.2), channel_id=1, source_target_pairs={{32,0},{232,8},{48,16},{248,24},{64,32},{8,40},{80,48},{24,56},{96... | collective-permute-start | bytes 589832 | tf_op jit(solution)/shard_map/ppermute | solution.py:260
  21.7 5.0 %collective-permute-start.7 = (f32[2,16,8,128]{3,2,1,0:T(8,128)S(1)}, f32[2,16,8,128]{3,2,1,0:T(8,128)S(1)}, u32[]{:S(2)}, u32[]{:S(2)}) collective-permute-start(f32[2,16,8,128]{3,2,1,0:T(8,128)S(1)} %pad_maximum_fusion.4), channel_id=1, source_target_pairs={{32,0},{232,8},{48,16},{248,24},{64,32},{8,40},{80,48},{24,56},{96... | collective-permute-start | bytes 393224 | tf_op jit(solution)/shard_map/ppermute | solution.py:260
  26.8 1.5 %collective-permute-start.8 = (f32[2,16,8,128]{3,2,1,0:T(8,128)S(1)}, f32[2,16,8,128]{3,2,1,0:T(8,128)S(1)}, u32[]{:S(2)}, u32[]{:S(2)}) collective-permute-start(f32[2,16,8,128]{3,2,1,0:T(8,128)S(1)} %collective-permute-done.7), channel_id=1, source_target_pairs={{8,0},{0,8},{24,16},{16,24},{40,32},{32,40},{56,48},{48,56},{72,64... | collective-permute-start | bytes 393224 | tf_op jit(solution)/shard_map/ppermute | solution.py:260
  27.2 4.5 %collective-permute-start.11 = (f32[3,16,8,128]{3,2,1,0:T(8,128)S(1)}, f32[3,16,8,128]{3,2,1,0:T(8,128)S(1)}, u32[]{:S(2)}, u32[]{:S(2)}) collective-permute-start(f32[3,16,8,128]{3,2,1,0:T(8,128)S(1)} %collective-permute-done.10), channel_id=1, source_target_pairs={{8,0},{0,8},{24,16},{16,24},{40,32},{32,40},{56,48},{48,56},{72,64... | collective-permute-start | bytes 589832 | tf_op jit(solution)/shard_map/ppermute | solution.py:260
  27.4 11.9 %collective-permute-start.15 = (f32[8,6,8,128]{3,2,1,0:T(8,128)S(1)}, f32[8,6,8,128]{3,2,1,0:T(8,128)S(1)}, u32[]{:S(2)}, u32[]{:S(2)}) collective-permute-start(f32[8,6,8,128]{3,2,1,0:T(8,128)S(1)} %get-tuple-element.43), channel_id=1, source_target_pairs={{1,0},{2,1},{3,2},{4,3},{5,4},{6,5},{7,6},{0,7},{9,8},{10,9},{11,1... | collective-permute-start | bytes 589832 | tf_op jit(solution)/shard_map/ppermute | solution.py:312
  28.3 11.1 %collective-permute-start.14 = (f32[8,6,8,128]{3,2,1,0:T(8,128)S(1)}, f32[8,6,8,128]{3,2,1,0:T(8,128)S(1)}, u32[]{:S(2)}, u32[]{:S(2)}) collective-permute-start(f32[8,6,8,128]{3,2,1,0:T(8,128)S(1)} %get-tuple-element.44), channel_id=1, source_target_pairs={{0,1},{1,2},{2,3},{3,4},{4,5},{5,6},{6,7},{7,0},{8,9},{9,10},{10,1... | collective-permute-start | bytes 589832 | tf_op jit(solution)/shard_map/ppermute | solution.py:312
  36.0 11.5 %collective-permute-start.12 = (f32[6,128,128]{2,1,0:T(8,128)S(1)}, f32[6,128,128]{2,1,0:T(8,128)S(1)}, u32[]{:S(2)}, u32[]{:S(2)}) collective-permute-start(f32[6,128,128]{2,1,0:T(8,128)S(1)} %get-tuple-element.31), channel_id=1, source_target_pairs={{0,1},{1,2},{2,3},{3,4},{4,5},{5,6},{6,7},{7,0},{8,9},{9,10},{10,1... | collective-permute-start | bytes 1179656 | tf_op jit(solution)/shard_map/ppermute | solution.py:316
  36.1 13.8 %collective-permute-start.13 = (f32[6,128,128]{2,1,0:T(8,128)S(1)}, f32[6,128,128]{2,1,0:T(8,128)S(1)}, u32[]{:S(2)}, u32[]{:S(2)}) collective-permute-start(f32[6,128,128]{2,1,0:T(8,128)S(1)} %get-tuple-element.32), channel_id=1, source_target_pairs={{1,0},{2,1},{3,2},{4,3},{5,4},{6,5},{7,6},{0,7},{9,8},{10,9},{11,1... | collective-permute-start | bytes 1179656 | tf_op jit(solution)/shard_map/ppermute | solution.py:315
  39.3 3.3 %collective-permute-start.17 = (f32[8,6,8,128]{3,2,1,0:T(8,128)S(1)}, f32[8,6,8,128]{3,2,1,0:T(8,128)S(1)}, u32[]{:S(2)}, u32[]{:S(2)}) collective-permute-start(f32[8,6,8,128]{3,2,1,0:T(8,128)S(1)} %collective-permute-done.15.ends_r), channel_id=1, source_target_pairs={{8,0},{0,8},{24,16},{16,24},{40,32},{32,40},{56,48},{48,56},{72,64... | collective-permute-start | bytes 589832 | tf_op jit(solution)/shard_map/ppermute | solution.py:260
  39.5 3.2 %collective-permute-start.16 = (f32[8,6,8,128]{3,2,1,0:T(8,128)S(1)}, f32[8,6,8,128]{3,2,1,0:T(8,128)S(1)}, u32[]{:S(2)}, u32[]{:S(2)}) collective-permute-start(f32[8,6,8,128]{3,2,1,0:T(8,128)S(1)} %collective-permute-done.14.ends_l), channel_id=1, source_target_pairs={{8,0},{0,8},{24,16},{16,24},{40,32},{32,40},{56,48},{48,56},{72,64... | collective-permute-start | bytes 589832 | tf_op jit(solution)/shard_map/ppermute | solution.py:260

commit v5 on v4

--- a/solution.py
+++ b/solution.py
@@ -291,7 +291,7 @@
         [block, in_order(part, twins[32:], 0), along, across, twins[:16], twins[16:32]], 0
     )
     half = jnp.where(core0, mine[2:3], mine[3:4])
-    gots = [of_band(part, lambda z, h, c: at(z + 1 - 2 * c, h, c)) for part in (mine[:2], jnp.concatenate([half, mine[4:]], 0))]
+    gots = [of_band(part, lambda z, h, c: at(z + 1 - 2 * c, h, c)) for part in (mine[:2], jnp.concatenate([half, mine[4:5]], 0), mine[5:])]
     got = jnp.concatenate(gots, 0)
     others = jnp.concatenate([flip(g) for g in gots], 0)
     xl, xr, others = lax.optimization_barrier((xl, xr, others))

time: 51.5 us -> 51.3 us (level)
  waiting for transfers between devices: 14.8 us -> 12.7 us
  starting transfers between devices: 24.1 us -> 26 us
    ppermute x12 -> x14, starting transfers between devices: 15.6 us -> 17.6 us  [of_band(): lax.ppermute(value, 'band', [(source(i // 4, i // 2 % 2, i % 2), i) for i...]
    ppermute x12 -> x14, waiting for transfers between devices: 6.89 us -> 5.01 us  [of_band(): lax.ppermute(value, 'band', [(source(i // 4, i // 2 % 2, i % 2), i) for i...]
  transfers between devices with their start and end apart: 18 -> 20, of which waited for: 8 -> 9; matrix products, arithmetic and copies ran while one was open for 4% -> 4% of each run, Pallas kernels for 17% -> 17%
where the time goes in v5:
time: 51.3 us; the launch traced here: 51.2 us
  starting transfers between devices  26 us (51%)
  waiting for transfers between devices  12.7 us (25%)
  Pallas kernels  10.2 us (20%)
  local copies, waits for them, and re-layouts  1.71 us (3%)
    ppermute x14, starting transfers between devices, of_band(): lax.ppermute(value, 'band', [(source(i // 4, i // 2 % 2, i % 2), i) for i...  17.6 us
    pallas_call x5, Pallas kernels, call(): pl.pallas_call(body, out_shape=tuple((jax.ShapeDtypeStruct(o, F32) for o...  8.82 us
    ppermute x14, waiting for transfers between devices, of_band(): lax.ppermute(value, 'band', [(source(i // 4, i // 2 % 2, i % 2), i) for i...  5.01 us
    ppermute x1, starting transfers between devices, shards(): lax.ppermute(ends[:, nx - W:], 'slab', up)  3.39 us
    ppermute x1, waiting for transfers between devices, shards(): xr = lax.ppermute(first, 'slab', down)  3.26 us
    ppermute x1, waiting for transfers between devices, shards(): far_r = lax.ppermute(to_left, 'slab', down)  2.2 us
    ppermute x1, starting transfers between devices, shards(): far_r = lax.ppermute(to_left, 'slab', down)  2.04 us
    slice x1, local copies, waits for them, and re-layouts, shards(): x[:12]  1.57 us
  transfers between devices with their start and end apart: 20, of which 9 were waited for; matrix products, arithmetic and copies ran while one was open for 4% of the time, Pallas kernels for 17%

profile of v5, /device:TPU:24, one launch (start us, length us, event | category | flops | bytes accessed | tf_op | source)
XLA Modules:
  0.0 51.2 jit_solution(23372655239397826)
XLA Ops:
  0.0 1.6 %slice_bitcast_fusion = (f32[12,128,128]{2,1,0:T(8,128)S(1)}, f32[12,128,128]{2,1,0:T(8,128)S(1)}) fusion(f32[1,16,128,128]{3,2,1,0:T(8,128)} %param.4), kind=kLoop, calls=%fused_computation | loop fusion | bytes 3145728 | tf_op jit(solution)/shard_map/slice | solution.py:280
  1.7 9.3 %collective-permute-start.2 = (f32[16,8,128]{2,1,0:T(8,128)S(1)}, f32[16,8,128]{2,1,0:T(8,128)S(1)}, u32[]{:S(2)}, u32[]{:S(2)}) collective-permute-start(f32[16,8,128]{2,1,0:T(8,128)S(1)} %maximum_select_fusion), channel_id=1, source_target_pairs={{112,0},{184,8},{96,16},{168,24},{144,32},{216,40},{128,48},{200,5... | collective-permute-start | bytes 196616 | tf_op jit(solution)/shard_map/ppermute | solution.py:260
  11.6 1.1 %collective-permute-start.4 = (f32[12,128,128]{2,1,0:T(8,128)S(1)}, f32[12,128,128]{2,1,0:T(8,128)S(1)}, u32[]{:S(2)}, u32[]{:S(2)}) collective-permute-start(f32[12,128,128]{2,1,0:T(8,128)S(1)} %get-tuple-element.25), channel_id=1, source_target_pairs={{0,1},{1,2},{2,3},{3,4},{4,5},{5,6},{6,7},{7,0},{8,9},{9,10},{10,1... | collective-permute-start | bytes 2359304 | tf_op jit(solution)/shard_map/ppermute | solution.py:284
  12.7 0.9 %collective-permute-start.5 = (f32[12,128,128]{2,1,0:T(8,128)S(1)}, f32[12,128,128]{2,1,0:T(8,128)S(1)}, u32[]{:S(2)}, u32[]{:S(2)}) collective-permute-start(f32[12,128,128]{2,1,0:T(8,128)S(1)} %get-tuple-element.26), channel_id=1, source_target_pairs={{1,0},{2,1},{3,2},{4,3},{5,4},{6,5},{7,6},{0,7},{9,8},{10,9},{11,1... | collective-permute-start | bytes 2359304 | tf_op jit(solution)/shard_map/ppermute | solution.py:285
  13.7 1.4 %shard_map.46.w1 = f32[16,128,128]{2,1,0:T(8,128)S(1)} custom-call(f32[16,128,128]{2,1,0:T(8,128)S(1)} %bitcast.29, bf16[256,256]{1,0:T(8,128)(2,1)S(1)} %copy-done.1, bf16[256,256]{1,0:T(8,128)(2,1)S(1)} %copy-done.2), custom_call_target="tpu_custom_call" | custom-call | flops 5242880000 | bytes 2359296 | tf_op jit(solution)/shard_map/pallas_call | solution.py:241
  15.1 1.4 %collective-permute-done.3 = f32[8,8,128]{2,1,0:T(8,128)S(1)} collective-permute-done((f32[8,8,128]{2,1,0:T(8,128)S(1)}, f32[8,8,128]{2,1,0:T(8,128)S(1)}, u32[]{:S(2)}, u32[]{:S(2)}) %collective-permute-start.3) | collective-permute-done | bytes 32800 | tf_op jit(solution)/shard_map/ppermute | solution.py:260
  16.5 0.6 %collective-permute-done.1 = f32[16,8,128]{2,1,0:T(8,128)S(1)} collective-permute-done((f32[16,8,128]{2,1,0:T(8,128)S(1)}, f32[16,8,128]{2,1,0:T(8,128)S(1)}, u32[]{:S(2)}, u32[]{:S(2)}) %collective-permute-start.1) | collective-permute-done | bytes 65568 | tf_op jit(solution)/shard_map/ppermute | solution.py:260
  17.8 0.7 %collective-permute-done.9 = f32[16,8,128]{2,1,0:T(8,128)S(1)} collective-permute-done((f32[16,8,128]{2,1,0:T(8,128)S(1)}, f32[16,8,128]{2,1,0:T(8,128)S(1)}, u32[]{:S(2)}, u32[]{:S(2)}) %collective-permute-start.9) | collective-permute-done | bytes 65568 | tf_op jit(solution)/shard_map/ppermute | solution.py:260
  18.5 2.9 %collective-permute-start.10 = (f32[2,16,8,128]{3,2,1,0:T(8,128)S(1)}, f32[2,16,8,128]{3,2,1,0:T(8,128)S(1)}, u32[]{:S(2)}, u32[]{:S(2)}) collective-permute-start(f32[2,16,8,128]{3,2,1,0:T(8,128)S(1)} %pad_maximum_fusion.4), channel_id=1, source_target_pairs={{32,0},{232,8},{48,16},{248,24},{64,32},{8,40},{80,48},{24,56},{96... | collective-permute-start | bytes 393224 | tf_op jit(solution)/shard_map/ppermute | solution.py:260
  21.5 0.9 %collective-permute-start.12 = (f32[1,16,8,128]{3,2,1,0:T(8,128)S(1)}, f32[1,16,8,128]{3,2,1,0:T(8,128)S(1)}, u32[]{:S(2)}, u32[]{:S(2)}) collective-permute-start(f32[1,16,8,128]{3,2,1,0:T(8,128)S(1)} %slice_bitcast_fusion.2), channel_id=1, source_target_pairs={{32,0},{232,8},{48,16},{248,24},{64,32},{8,40},{80,48},{24,56},{96... | collective-permute-start | bytes 196616 | tf_op jit(solution)/shard_map/ppermute | solution.py:260
  22.4 2.3 %collective-permute-start.7 = (f32[2,16,8,128]{3,2,1,0:T(8,128)S(1)}, f32[2,16,8,128]{3,2,1,0:T(8,128)S(1)}, u32[]{:S(2)}, u32[]{:S(2)}) collective-permute-start(f32[2,16,8,128]{3,2,1,0:T(8,128)S(1)} %pad_maximum_fusion.3), channel_id=1, source_target_pairs={{32,0},{232,8},{48,16},{248,24},{64,32},{8,40},{80,48},{24,56},{96... | collective-permute-start | bytes 393224 | tf_op jit(solution)/shard_map/ppermute | solution.py:260
  24.8 1.0 %collective-permute-done.12 = f32[1,16,8,128]{3,2,1,0:T(8,128)S(1)} collective-permute-done((f32[1,16,8,128]{3,2,1,0:T(8,128)S(1)}, f32[1,16,8,128]{3,2,1,0:T(8,128)S(1)}, u32[]{:S(2)}, u32[]{:S(2)}) %collective-permute-start.12) | collective-permute-done | bytes 65568 | tf_op jit(solution)/shard_map/ppermute | solution.py:260
  26.3 1.2 %collective-permute-done.7 = f32[2,16,8,128]{3,2,1,0:T(8,128)S(1)} collective-permute-done((f32[2,16,8,128]{3,2,1,0:T(8,128)S(1)}, f32[2,16,8,128]{3,2,1,0:T(8,128)S(1)}, u32[]{:S(2)}, u32[]{:S(2)}) %collective-permute-start.7) | collective-permute-done | bytes 131104 | tf_op jit(solution)/shard_map/ppermute | solution.py:260
  27.6 0.8 %collective-permute-start.17 = (f32[8,6,8,128]{3,2,1,0:T(8,128)S(1)}, f32[8,6,8,128]{3,2,1,0:T(8,128)S(1)}, u32[]{:S(2)}, u32[]{:S(2)}) collective-permute-start(f32[8,6,8,128]{3,2,1,0:T(8,128)S(1)} %get-tuple-element.43), channel_id=1, source_target_pairs={{1,0},{2,1},{3,2},{4,3},{5,4},{6,5},{7,6},{0,7},{9,8},{10,9},{11,1... | collective-permute-start | bytes 589832 | tf_op jit(solution)/shard_map/ppermute | solution.py:312
  28.4 3.4 %collective-permute-start.16 = (f32[8,6,8,128]{3,2,1,0:T(8,128)S(1)}, f32[8,6,8,128]{3,2,1,0:T(8,128)S(1)}, u32[]{:S(2)}, u32[]{:S(2)}) collective-permute-start(f32[8,6,8,128]{3,2,1,0:T(8,128)S(1)} %get-tuple-element.44), channel_id=1, source_target_pairs={{0,1},{1,2},{2,3},{3,4},{4,5},{5,6},{6,7},{7,0},{8,9},{9,10},{10,1... | collective-permute-start | bytes 589832 | tf_op jit(solution)/shard_map/ppermute | solution.py:312
  31.9 3.3 %collective-permute-done.5.xr = f32[12,128,128]{2,1,0:T(8,128)S(1)} collective-permute-done((f32[12,128,128]{2,1,0:T(8,128)S(1)}, f32[12,128,128]{2,1,0:T(8,128)S(1)}, u32[]{:S(2)}, u32[]{:S(2)}) %collective-permute-start.5) | collective-permute-done | bytes 786464 | tf_op jit(solution)/shard_map/ppermute | solution.py:285
  35.2 0.7 %shard_map.48 = (f32[16,128,128]{2,1,0:T(8,128)S(1)}, f32[6,128,128]{2,1,0:T(8,128)S(1)}, f32[6,128,128]{2,1,0:T(8,128)S(1)}) custom-call(f32[16,128,128]{2,1,0:T(8,128)S(1)} %bitcast.30, f32[16,128,128]{2,1,0:T(8,128)S(1)} %shard_map.46.w1, f32[12,128,128]{2,1,0:T(8,128)S(1)} %collective-permute-done.4.xl, f32[12,128,128]{2,1,0:T(8,128)S(1)} %collective-permute-done.5.xr, ...), custom_call_target="tpu_custom_call" | custom-call | tf_op jit(solution)/shard_map/pallas_call | solution.py:241
  36.1 2.0 %collective-permute-start.15 = (f32[6,128,128]{2,1,0:T(8,128)S(1)}, f32[6,128,128]{2,1,0:T(8,128)S(1)}, u32[]{:S(2)}, u32[]{:S(2)}) collective-permute-start(f32[6,128,128]{2,1,0:T(8,128)S(1)} %get-tuple-element.32), channel_id=1, source_target_pairs={{1,0},{2,1},{3,2},{4,3},{5,4},{6,5},{7,6},{0,7},{9,8},{10,9},{11,1... | collective-permute-start | bytes 1179656 | tf_op jit(solution)/shard_map/ppermute | solution.py:315
  38.1 1.2 %collective-permute-done.17.ends_r = f32[8,6,8,128]{3,2,1,0:T(8,128)S(1)} collective-permute-done((f32[8,6,8,128]{3,2,1,0:T(8,128)S(1)}, f32[8,6,8,128]{3,2,1,0:T(8,128)S(1)}, u32[]{:S(2)}, u32[]{:S(2)}) %collective-permute-start.17) | collective-permute-done | bytes 196640 | tf_op jit(solution)/shard_map/ppermute | solution.py:312
  39.8 2.8 %shard_map.49 = (f32[12,128,128]{2,1,0:T(8,128)S(1)}, f32[16,128,128]{2,1,0:T(8,128)S(1)}) custom-call(f32[16,128,128]{2,1,0:T(8,128)S(1)} %bitcast.31, f32[12,128,128]{2,1,0:T(8,128)S(1)} %collective-permute-done.4.xl, f32[12,128,128]{2,1,0:T(8,128)S(1)} %collective-permute-done.5.xr, f32[16,128,128]{2,1,0:T(8,128)S(1)} %get-tuple-element.33.y1, ...), custom_call_target="tpu_custom_call" | custom-call | tf_op jit(solution)/shard_map/pallas_call | solution.py:241
  42.7 3.8 %shard_map.50 = (f32[6,128,128]{2,1,0:T(8,128)S(1)}, f32[6,128,128]{2,1,0:T(8,128)S(1)}, f32[16,128,128]{2,1,0:T(8,128)S(1)}) custom-call(f32[12,128,128]{2,1,0:T(8,128)S(1)} %collective-permute-done.4.xl, f32[12,128,128]{2,1,0:T(8,128)S(1)} %collective-permute-done.5.xr, f32[16,128,128]{2,1,0:T(8,128)S(1)} %get-tuple-element.33.y1, ...), custom_call_target="tpu_custom_call" | custom-call | tf_op jit(solution)/shard_map/pallas_call | solution.py:241
  46.5 1.0 %collective-permute-done.14.far_l = f32[6,128,128]{2,1,0:T(8,128)S(1)} collective-permute-done((f32[6,128,128]{2,1,0:T(8,128)S(1)}, f32[6,128,128]{2,1,0:T(8,128)S(1)}, u32[]{:S(2)}, u32[]{:S(2)}) %collective-permute-start.14) | collective-permute-done | bytes 393248 | tf_op jit(solution)/shard_map/ppermute | solution.py:316
  47.5 2.2 %collective-permute-done.15.far_r = f32[6,128,128]{2,1,0:T(8,128)S(1)} collective-permute-done((f32[6,128,128]{2,1,0:T(8,128)S(1)}, f32[6,128,128]{2,1,0:T(8,128)S(1)}, u32[]{:S(2)}, u32[]{:S(2)}) %collective-permute-start.15) | collective-permute-done | bytes 393248 | tf_op jit(solution)/shard_map/ppermute | solution.py:315
  49.7 1.4 %shard_map.51 = f32[16,128,128]{2,1,0:T(8,128)} custom-call(f32[6,128,128]{2,1,0:T(8,128)S(1)} %collective-permute-done.14.far_l, f32[6,128,128]{2,1,0:T(8,128)S(1)} %collective-permute-done.15.far_r, f32[6,128,128]{2,1,0:T(8,128)S(1)} %get-tuple-element.36.y2l, f32[6,128,128]{2,1,0:T(8,128)S(1)} %get-tuple-element.37.y2r, ...), custom_call_target="tpu_custom_call" | custom-call | flops 2621440 | bytes 2097152 | tf_op jit(solution)/shard_map/pallas_call | solution.py:328
  (53 shorter events, 2.8 us)
Async XLA Ops:
  0.0 13.7 %copy-start = (f32[1,16,128,128]{3,2,1,0:T(8,128)S(1)}, f32[1,16,128,128]{3,2,1,0:T(8,128)}, u32[]{:S(2)}) copy-start(f32[1,16,128,128]{3,2,1,0:T(8,128)} %param.4) | copy-start | bytes 3145732
  0.0 1.6 %collective-permute-start = (f32[16,4,128]{2,1,0:T(4,128)}, f32[16,4,128]{2,1,0:T(4,128)S(1)}, u32[]{:S(2)}, u32[]{:S(2)}) collective-permute-start(f32[16,4,128]{2,1,0:T(4,128)} %param.5), channel_id=1, source_target_pairs={{8,0},{0,8},{24,16},{16,24},{40,32},{32,40},{56,48},{48,56},{72,64... | collective-permute-start | bytes 98312 | tf_op jit(solution)/shard_map/ppermute | solution.py:260
  0.0 1.6 %copy-start.3 = (f32[16,4,128]{2,1,0:T(4,128)S(1)}, f32[16,4,128]{2,1,0:T(4,128)}, u32[]{:S(2)}) copy-start(f32[16,4,128]{2,1,0:T(4,128)} %param.5) | copy-start | bytes 98308
  1.6 12.1 %copy-start.2 = (bf16[256,256]{1,0:T(8,128)(2,1)S(1)}, bf16[256,256]{1,0:T(8,128)(2,1)}, u32[]{:S(2)}) copy-start(bf16[256,256]{1,0:T(8,128)(2,1)} %constant.24.clone.right) | copy-start | bytes 393220
  1.6 12.1 %copy-start.1 = (bf16[256,256]{1,0:T(8,128)(2,1)S(1)}, bf16[256,256]{1,0:T(8,128)(2,1)}, u32[]{:S(2)}) copy-start(bf16[256,256]{1,0:T(8,128)(2,1)} %constant.25.clone.left) | copy-start | bytes 393220
  1.7 14.8 %collective-permute-start.2 = (f32[16,8,128]{2,1,0:T(8,128)S(1)}, f32[16,8,128]{2,1,0:T(8,128)S(1)}, u32[]{:S(2)}, u32[]{:S(2)}) collective-permute-start(f32[16,8,128]{2,1,0:T(8,128)S(1)} %maximum_select_fusion), channel_id=1, source_target_pairs={{112,0},{184,8},{96,16},{168,24},{144,32},{216,40},{128,48},{200,5... | collective-permute-start | bytes 196616 | tf_op jit(solution)/shard_map/ppermute | solution.py:260
  11.0 6.2 %collective-permute-start.1 = (f32[16,8,128]{2,1,0:T(8,128)S(1)}, f32[16,8,128]{2,1,0:T(8,128)S(1)}, u32[]{:S(2)}, u32[]{:S(2)}) collective-permute-start(f32[16,8,128]{2,1,0:T(8,128)S(1)} %maximum_select_fusion), channel_id=1, source_target_pairs={{96,0},{168,8},{112,16},{184,24},{128,32},{200,40},{144,48},{216,5... | collective-permute-start | bytes 196616 | tf_op jit(solution)/shard_map/ppermute | solution.py:260
  11.1 5.4 %collective-permute-start.3 = (f32[8,8,128]{2,1,0:T(8,128)S(1)}, f32[8,8,128]{2,1,0:T(8,128)S(1)}, u32[]{:S(2)}, u32[]{:S(2)}) collective-permute-start(f32[8,8,128]{2,1,0:T(8,128)S(1)} %slice_select_fusion), channel_id=1, source_target_pairs={{16,0},{24,8},{0,16},{8,24},{48,32},{56,40},{32,48},{40,56},{80,64... | collective-permute-start | bytes 98312 | tf_op jit(solution)/shard_map/ppermute | solution.py:260
  11.6 20.2 %collective-permute-start.4 = (f32[12,128,128]{2,1,0:T(8,128)S(1)}, f32[12,128,128]{2,1,0:T(8,128)S(1)}, u32[]{:S(2)}, u32[]{:S(2)}) collective-permute-start(f32[12,128,128]{2,1,0:T(8,128)S(1)} %get-tuple-element.25), channel_id=1, source_target_pairs={{0,1},{1,2},{2,3},{3,4},{4,5},{5,6},{6,7},{7,0},{8,9},{9,10},{10,1... | collective-permute-start | bytes 2359304 | tf_op jit(solution)/shard_map/ppermute | solution.py:284
  12.7 22.4 %collective-permute-start.5 = (f32[12,128,128]{2,1,0:T(8,128)S(1)}, f32[12,128,128]{2,1,0:T(8,128)S(1)}, u32[]{:S(2)}, u32[]{:S(2)}) collective-permute-start(f32[12,128,128]{2,1,0:T(8,128)S(1)} %get-tuple-element.26), channel_id=1, source_target_pairs={{1,0},{2,1},{3,2},{4,3},{5,4},{6,5},{7,6},{0,7},{9,8},{10,9},{11,1... | collective-permute-start | bytes 2359304 | tf_op jit(solution)/shard_map/ppermute | solution.py:285
  17.2 1.3 %collective-permute-start.9 = (f32[16,8,128]{2,1,0:T(8,128)S(1)}, f32[16,8,128]{2,1,0:T(8,128)S(1)}, u32[]{:S(2)}, u32[]{:S(2)}) collective-permute-start(f32[16,8,128]{2,1,0:T(8,128)S(1)} %slice.52), channel_id=1, source_target_pairs={{8,0},{0,8},{24,16},{16,24},{40,32},{32,40},{56,48},{48,56},{72,64... | collective-permute-start | bytes 196616 | tf_op jit(solution)/shard_map/ppermute | solution.py:260
  17.4 4.1 %collective-permute-start.6 = (f32[24,8,128]{2,1,0:T(8,128)S(1)}, f32[24,8,128]{2,1,0:T(8,128)S(1)}, u32[]{:S(2)}, u32[]{:S(2)}) collective-permute-start(f32[24,8,128]{2,1,0:T(8,128)S(1)} %slice.50), channel_id=1, source_target_pairs={{8,0},{0,8},{24,16},{16,24},{40,32},{32,40},{56,48},{48,56},{72,64... | collective-permute-start | bytes 294920 | tf_op jit(solution)/shard_map/ppermute | solution.py:260
  18.5 7.5 %collective-permute-start.10 = (f32[2,16,8,128]{3,2,1,0:T(8,128)S(1)}, f32[2,16,8,128]{3,2,1,0:T(8,128)S(1)}, u32[]{:S(2)}, u32[]{:S(2)}) collective-permute-start(f32[2,16,8,128]{3,2,1,0:T(8,128)S(1)} %pad_maximum_fusion.4), channel_id=1, source_target_pairs={{32,0},{232,8},{48,16},{248,24},{64,32},{8,40},{80,48},{24,56},{96... | collective-permute-start | bytes 393224 | tf_op jit(solution)/shard_map/ppermute | solution.py:260
  21.5 4.3 %collective-permute-start.12 = (f32[1,16,8,128]{3,2,1,0:T(8,128)S(1)}, f32[1,16,8,128]{3,2,1,0:T(8,128)S(1)}, u32[]{:S(2)}, u32[]{:S(2)}) collective-permute-start(f32[1,16,8,128]{3,2,1,0:T(8,128)S(1)} %slice_bitcast_fusion.2), channel_id=1, source_target_pairs={{32,0},{232,8},{48,16},{248,24},{64,32},{8,40},{80,48},{24,56},{96... | collective-permute-start | bytes 196616 | tf_op jit(solution)/shard_map/ppermute | solution.py:260
  22.4 5.0 %collective-permute-start.7 = (f32[2,16,8,128]{3,2,1,0:T(8,128)S(1)}, f32[2,16,8,128]{3,2,1,0:T(8,128)S(1)}, u32[]{:S(2)}, u32[]{:S(2)}) collective-permute-start(f32[2,16,8,128]{3,2,1,0:T(8,128)S(1)} %pad_maximum_fusion.3), channel_id=1, source_target_pairs={{32,0},{232,8},{48,16},{248,24},{64,32},{8,40},{80,48},{24,56},{96... | collective-permute-start | bytes 393224 | tf_op jit(solution)/shard_map/ppermute | solution.py:260
  25.8 1.8 %collective-permute-start.13 = (f32[1,16,8,128]{3,2,1,0:T(8,128)S(1)}, f32[1,16,8,128]{3,2,1,0:T(8,128)S(1)}, u32[]{:S(2)}, u32[]{:S(2)}) collective-permute-start(f32[1,16,8,128]{3,2,1,0:T(8,128)S(1)} %collective-permute-done.12), channel_id=1, source_target_pairs={{8,0},{0,8},{24,16},{16,24},{40,32},{32,40},{56,48},{48,56},{72,64... | collective-permute-start | bytes 196616 | tf_op jit(solution)/shard_map/ppermute | solution.py:260
  26.0 2.4 %collective-permute-start.11 = (f32[2,16,8,128]{3,2,1,0:T(8,128)S(1)}, f32[2,16,8,128]{3,2,1,0:T(8,128)S(1)}, u32[]{:S(2)}, u32[]{:S(2)}) collective-permute-start(f32[2,16,8,128]{3,2,1,0:T(8,128)S(1)} %collective-permute-done.10), channel_id=1, source_target_pairs={{8,0},{0,8},{24,16},{16,24},{40,32},{32,40},{56,48},{48,56},{72,64... | collective-permute-start | bytes 393224 | tf_op jit(solution)/shard_map/ppermute | solution.py:260
  27.5 4.4 %collective-permute-start.8 = (f32[2,16,8,128]{3,2,1,0:T(8,128)S(1)}, f32[2,16,8,128]{3,2,1,0:T(8,128)S(1)}, u32[]{:S(2)}, u32[]{:S(2)}) collective-permute-start(f32[2,16,8,128]{3,2,1,0:T(8,128)S(1)} %collective-permute-done.7), channel_id=1, source_target_pairs={{8,0},{0,8},{24,16},{16,24},{40,32},{32,40},{56,48},{48,56},{72,64... | collective-permute-start | bytes 393224 | tf_op jit(solution)/shard_map/ppermute | solution.py:260
  27.6 11.7 %collective-permute-start.17 = (f32[8,6,8,128]{3,2,1,0:T(8,128)S(1)}, f32[8,6,8,128]{3,2,1,0:T(8,128)S(1)}, u32[]{:S(2)}, u32[]{:S(2)}) collective-permute-start(f32[8,6,8,128]{3,2,1,0:T(8,128)S(1)} %get-tuple-element.43), channel_id=1, source_target_pairs={{1,0},{2,1},{3,2},{4,3},{5,4},{6,5},{7,6},{0,7},{9,8},{10,9},{11,1... | collective-permute-start | bytes 589832 | tf_op jit(solution)/shard_map/ppermute | solution.py:312
  28.4 11.0 %collective-permute-start.16 = (f32[8,6,8,128]{3,2,1,0:T(8,128)S(1)}, f32[8,6,8,128]{3,2,1,0:T(8,128)S(1)}, u32[]{:S(2)}, u32[]{:S(2)}) collective-permute-start(f32[8,6,8,128]{3,2,1,0:T(8,128)S(1)} %get-tuple-element.44), channel_id=1, source_target_pairs={{0,1},{1,2},{2,3},{3,4},{4,5},{5,6},{6,7},{7,0},{8,9},{9,10},{10,1... | collective-permute-start | bytes 589832 | tf_op jit(solution)/shard_map/ppermute | solution.py:312
  36.0 11.5 %collective-permute-start.14 = (f32[6,128,128]{2,1,0:T(8,128)S(1)}, f32[6,128,128]{2,1,0:T(8,128)S(1)}, u32[]{:S(2)}, u32[]{:S(2)}) collective-permute-start(f32[6,128,128]{2,1,0:T(8,128)S(1)} %get-tuple-element.31), channel_id=1, source_target_pairs={{0,1},{1,2},{2,3},{3,4},{4,5},{5,6},{6,7},{7,0},{8,9},{9,10},{10,1... | collective-permute-start | bytes 1179656 | tf_op jit(solution)/shard_map/ppermute | solution.py:316
  36.1 13.6 %collective-permute-start.15 = (f32[6,128,128]{2,1,0:T(8,128)S(1)}, f32[6,128,128]{2,1,0:T(8,128)S(1)}, u32[]{:S(2)}, u32[]{:S(2)}) collective-permute-start(f32[6,128,128]{2,1,0:T(8,128)S(1)} %get-tuple-element.32), channel_id=1, source_target_pairs={{1,0},{2,1},{3,2},{4,3},{5,4},{6,5},{7,6},{0,7},{9,8},{10,9},{11,1... | collective-permute-start | bytes 1179656 | tf_op jit(solution)/shard_map/ppermute | solution.py:315
  39.3 3.3 %collective-permute-start.19 = (f32[8,6,8,128]{3,2,1,0:T(8,128)S(1)}, f32[8,6,8,128]{3,2,1,0:T(8,128)S(1)}, u32[]{:S(2)}, u32[]{:S(2)}) collective-permute-start(f32[8,6,8,128]{3,2,1,0:T(8,128)S(1)} %collective-permute-done.17.ends_r), channel_id=1, source_target_pairs={{8,0},{0,8},{24,16},{16,24},{40,32},{32,40},{56,48},{48,56},{72,64... | collective-permute-start | bytes 589832 | tf_op jit(solution)/shard_map/ppermute | solution.py:260
  39.5 3.2 %collective-permute-start.18 = (f32[8,6,8,128]{3,2,1,0:T(8,128)S(1)}, f32[8,6,8,128]{3,2,1,0:T(8,128)S(1)}, u32[]{:S(2)}, u32[]{:S(2)}) collective-permute-start(f32[8,6,8,128]{3,2,1,0:T(8,128)S(1)} %collective-permute-done.16.ends_l), channel_id=1, source_target_pairs={{8,0},{0,8},{24,16},{16,24},{40,32},{32,40},{56,48},{48,56},{72,64... | collective-permute-start | bytes 589832 | tf_op jit(solution)/shard_map/ppermute | solution.py:260
